TPU v7x, 512 devices: a whole 4x4x16 slice. The times are simulated.
512 devices in a mesh: seq: 16 (over z), tp: 8 (over y, core), dp: 4 (over x).
Axes of the slice: x: 4, y: 4, z: 16, core: 2. Of those that a mesh axis runs over, the one named last changes fastest.
Arguments:
- x_in: bfloat16 [4, 2048, 4096], P('dp', 'seq', 'tp'), may hold values from -7 to 7
- dt_in: bfloat16 [4, 2048, 4096], P('dp', 'seq', 'tp'), may hold values from -2 to 9
- b_in: bfloat16 [4, 16, 2048], P('dp', None, 'seq'), may hold values from -1 to 3
- c_in: bfloat16 [4, 16, 2048], P('dp', None, 'seq'), may hold values from -4 to 4
- dy_in: bfloat16 [4, 2048, 4096], P('dp', 'seq', 'tp'), may hold values from -6 to 6
- a_log: float32 [16, 4096], P(None, 'tp'), may hold values from 0 to 2.77
- d_skip: float32 [4096], P('tp'), may hold values from 0.1 to 1.9
- dt_bias: float32 [4096], P('tp'), may hold values from -14 to -2
- q_in: bfloat16 [4, 2048, 4096], P('dp', 'seq', 'tp'), may hold values from -8 to 8
- k_in: bfloat16 [4, 2048, 1024], P('dp', 'seq', 'tp'), may hold values from -6 to 6
- value_input: bfloat16 [4, 2048, 1024], P('dp', 'seq', 'tp'), may hold values from -6 to 6
- dout_in: bfloat16 [4, 2048, 4096], P('dp', 'seq', 'tp'), may hold values from -6 to 6
- doc_lengths: int32 [4, 8], P('dp'), may hold values from 1 to 1600, 2048 in all within a row
- plan: int32 [4, 64], P('dp'), may hold values from 0 to 63, each once within a row
Outputs:
- ssm_out: bfloat16 [4, 2048, 4096], P('dp', 'seq', 'tp')
- x_grad: bfloat16 [4, 2048, 4096], P('dp', 'seq', 'tp')
- dt_grad: bfloat16 [4, 2048, 4096], P('dp', 'seq', 'tp')
- b_grad: float32 [4, 16, 2048], P('dp', None, 'seq')
- c_grad: float32 [4, 16, 2048], P('dp', None, 'seq')
- a_log_grad: float32 [16, 4096], P(None, 'tp')
- d_skip_grad: float32 [4096], P('tp')
- dt_bias_grad: float32 [4096], P('tp')
- attn_out: bfloat16 [4, 2048, 4096], P('dp', 'seq', 'tp')
- query_gradient: bfloat16 [4, 2048, 4096], P('dp', 'seq', 'tp')
- key_gradient: bfloat16 [4, 2048, 1024], P('dp', 'seq', 'tp')
- value_gradient: bfloat16 [4, 2048, 1024], P('dp', 'seq', 'tp')
All inputs are finite; a program needn't handle non-finite values.
Results may differ from a plain program's by a relative error of at most 0.04.
Values may be sent and summed in bfloat16 or wider, within the bound.
No kernel may reach another device: no remote copies, remote signals or barrier semaphores. Data moves between devices by JAX's collectives and lax.ppermute only.
A program may use at most 64 MiB of HBM per device.

v0:
```python
import jax
import jax.numpy as jnp
from jax import lax
from jax.sharding import PartitionSpec as P

NS = 16
HEAD_SIZE = 128
SUB = 16
CB = 128
BLOCK = 32


NEG_FILL = -1e30


def carried_in(value, axis, join, neutral, backward):
    count, mine = (lax.axis_size(axis), lax.axis_index(axis))
    pieces = jax.tree.map(lambda part: lax.all_gather(part, axis), value)
    if backward:
        pieces = jax.tree.map(lambda part: part[::-1], pieces)
        mine = count - 1 - mine
    total = jax.tree.map(
        lambda part, zero: jnp.full_like(part, 0) + jnp.asarray(zero, part.dtype), value, neutral
    )

    def turn(position, total):
        longer = join(total, jax.tree.map(lambda part: part[position], pieces))
        return jax.tree.map(lambda new, old: jnp.where(position < mine, new, old), longer, total)

    return lax.fori_loop(0, count - 1, turn, total)


def pair_combine(earlier, later):
    return (earlier[0] * later[0], later[0] * earlier[1] + later[1])


def keep_state(state):
    return state


def block_scan(decay, drive):
    groups = decay.shape[0] // SUB
    decay_groups = decay.reshape((groups, SUB) + decay.shape[1:])
    drive_groups = drive.reshape((groups, SUB) + drive.shape[1:])
    factors = [decay_groups[:, 0]]
    states = [drive_groups[:, 0]]
    for position in range(1, SUB):
        factors.append(factors[-1] * decay_groups[:, position])
        states.append(decay_groups[:, position] * states[-1] + drive_groups[:, position])
    factor_in = jnp.stack(factors, 1)
    state_in = jnp.stack(states, 1)
    end_factor, end_state = lax.associative_scan(pair_combine, (factor_in[:, -1], state_in[:, -1]))
    lead_factor = jnp.concatenate([jnp.ones_like(end_factor[:1]), end_factor[:-1]], 0)
    lead_state = jnp.concatenate([jnp.zeros_like(end_state[:1]), end_state[:-1]], 0)
    factor_all = factor_in * lead_factor[:, None]
    state_all = state_in + factor_in * lead_state[:, None]
    return (factor_all.reshape(decay.shape), state_all.reshape(decay.shape))


def to_wide(stacked):
    return jnp.transpose(stacked, (1, 0, 2)).reshape(
        stacked.shape[1], stacked.shape[0] * stacked.shape[2]
    )


def piece_grads(query_tensor, d_att, lse, rowdot, key_tensor, value_tensor, mask, scale):
    scores = (
        jnp.einsum("qhgd,khd->hgqk", query_tensor, key_tensor, preferred_element_type=jnp.float32)
        * scale
    )
    probs = jnp.where(mask, jnp.exp(scores - lse[..., None]), 0.0)
    d_prob = jnp.einsum("qhgd,khd->hgqk", d_att, value_tensor, preferred_element_type=jnp.float32)
    d_score = (probs * (d_prob - rowdot[..., None])).astype(jnp.bfloat16)
    count = key_tensor.shape[0]
    kv_count = key_tensor.shape[1]
    results = []
    results.append(
        jnp.einsum("hgqk,khd->hgqd", d_score, key_tensor, preferred_element_type=jnp.float32)
        * scale
    )
    probs_half = probs.astype(jnp.bfloat16)
    value_part = jnp.einsum("hgqk,qhgd->khd", probs_half, d_att, preferred_element_type=jnp.float32)
    key_part = (
        jnp.einsum("hgqk,qhgd->khd", d_score, query_tensor, preferred_element_type=jnp.float32)
        * scale
    )
    results.append(key_part.reshape(count, kv_count * HEAD_SIZE))
    results.append(value_part.reshape(count, kv_count * HEAD_SIZE))
    return results


def on_device(
    x_in,
    dt_in,
    b_in,
    c_in,
    dy_in,
    a_log,
    d_skip,
    dt_bias,
    q_in,
    k_in,
    value_input,
    dout_in,
    doc_lengths,
    plan,
):
    seq_count = lax.axis_size("seq")
    own = lax.axis_index("seq")
    local = x_in.shape[1]
    row_tokens = local * seq_count
    lengths = doc_lengths[0]
    ends = jnp.cumsum(lengths)
    starts = ends - lengths
    assignment_table = jnp.arange(row_tokens, dtype=jnp.int32)
    doc_of = jnp.sum((assignment_table[:, None] >= ends[None, :]).astype(jnp.int32), axis=1)
    first_row = jnp.any(assignment_table[:, None] == starts[None, :], axis=1)
    keep = lax.dynamic_slice_in_dim(1.0 - first_row.astype(jnp.float32), own * local, local)
    width = x_in.shape[2]
    blocks = width // CB
    b_rows = b_in[0].astype(jnp.float32).T
    c_rows = c_in[0].astype(jnp.float32).T
    rate_full = -jnp.exp(a_log)

    def prepare(index):
        lower = index * CB
        inputs = lax.dynamic_slice_in_dim(x_in[0], lower, CB, 1).astype(jnp.float32)
        raw = lax.dynamic_slice_in_dim(dt_in[0], lower, CB, 1).astype(jnp.float32)
        raw = raw + lax.dynamic_slice_in_dim(dt_bias, lower, CB, 0)
        upstream = lax.dynamic_slice_in_dim(dy_in[0], lower, CB, 1).astype(jnp.float32)
        rates = lax.dynamic_slice_in_dim(rate_full, lower, CB, 1)
        delta = jax.nn.softplus(raw)
        decay = jnp.exp(delta[:, None, :] * rates[None]) * keep[:, None, None]
        drive = delta[:, None, :] * b_rows[:, :, None] * inputs[:, None, :]
        onward_factor, onward_state = block_scan(decay, drive)
        source = c_rows[:, :, None] * upstream[:, None, :]
        shifted = jnp.concatenate([decay[1:], jnp.ones_like(decay[:1])], 0)
        back_factor, back_state = block_scan(jnp.flip(shifted, 0), jnp.flip(source, 0))
        return (
            inputs,
            raw,
            upstream,
            rates,
            delta,
            decay,
            onward_factor,
            onward_state,
            jnp.flip(back_factor, 0),
            jnp.flip(back_state, 0),
        )

    def summarize(index):
        parts = prepare(index)
        decay = parts[5]
        return (parts[6][-1], parts[7][-1], decay[0] * parts[8][0], decay[0] * parts[9][0])

    summary = lax.map(summarize, jnp.arange(blocks, dtype=jnp.int32))
    onward_end = to_wide(summary[0])
    onward_sum = to_wide(summary[1])
    backward_end = to_wide(summary[2])
    backward_sum = to_wide(summary[3])
    identity = (jnp.ones_like(onward_end), jnp.zeros_like(onward_sum))
    carried = carried_in((onward_end, onward_sum), "seq", pair_combine, identity, False)[1]
    returned = carried_in((backward_end, backward_sum), "seq", pair_combine, identity, True)[1]

    def accumulate(index, totals):
        (
            inputs,
            raw,
            upstream,
            rates,
            delta,
            decay,
            onward_factor,
            onward_state,
            back_factor,
            back_state,
        ) = prepare(index)
        lower = index * CB
        entering = lax.dynamic_slice_in_dim(carried, lower, CB, 1)
        arriving = lax.dynamic_slice_in_dim(returned, lower, CB, 1)
        skip = lax.dynamic_slice_in_dim(d_skip, lower, CB, 0)
        states = onward_state + onward_factor * entering[None]
        adjoint = back_state + back_factor * arriving[None]
        before = jnp.concatenate([entering[None], states[:-1]], 0)
        output = jnp.sum(c_rows[:, :, None] * states, axis=1) + skip * inputs
        input_grad = jnp.sum(adjoint * b_rows[:, :, None], axis=1) * delta + skip * upstream
        delta_grad = jnp.sum(
            adjoint * (b_rows[:, :, None] * inputs[:, None, :] + rates[None] * decay * before),
            axis=1,
        )
        raw_grad = delta_grad * jax.nn.sigmoid(raw)
        b_part = jnp.sum(adjoint * (delta * inputs)[:, None, :], axis=2)
        c_part = jnp.sum(upstream[:, None, :] * states, axis=2)
        rate_part = rates * jnp.sum(adjoint * decay * delta[:, None, :] * before, axis=0)
        output_all, input_all, raw_all, b_total, c_total, rate_all, skip_all, bias_all = totals
        return (
            lax.dynamic_update_slice_in_dim(output_all, output.astype(jnp.bfloat16), lower, 1),
            lax.dynamic_update_slice_in_dim(input_all, input_grad.astype(jnp.bfloat16), lower, 1),
            lax.dynamic_update_slice_in_dim(raw_all, raw_grad.astype(jnp.bfloat16), lower, 1),
            b_total + b_part,
            c_total + c_part,
            lax.dynamic_update_slice_in_dim(rate_all, rate_part, lower, 1),
            lax.dynamic_update_slice_in_dim(skip_all, jnp.sum(upstream * inputs, axis=0), lower, 0),
            lax.dynamic_update_slice_in_dim(bias_all, jnp.sum(raw_grad, axis=0), lower, 0),
        )

    starting = (
        jnp.zeros((local, width), jnp.bfloat16),
        jnp.zeros((local, width), jnp.bfloat16),
        jnp.zeros((local, width), jnp.bfloat16),
        jnp.zeros((local, NS), jnp.float32),
        jnp.zeros((local, NS), jnp.float32),
        jnp.zeros((NS, width), jnp.float32),
        jnp.zeros((width,), jnp.float32),
        jnp.zeros((width,), jnp.float32),
    )
    output_all, input_all, raw_all, b_total, c_total, rate_all, skip_all, bias_all = lax.fori_loop(
        0, blocks, accumulate, starting
    )
    b_sum, c_sum = lax.psum((b_total, c_total), "tp")
    rate_sum, skip_sum, bias_sum = lax.psum((rate_all, skip_all, bias_all), ("seq", "dp"))
    head_count = q_in.shape[2] // HEAD_SIZE
    kv_count = k_in.shape[2] // HEAD_SIZE
    query_group = head_count // kv_count
    scale = HEAD_SIZE ** (-0.5)
    per_device = local // BLOCK
    all_queries = lax.all_gather(q_in, "seq", axis=1, tiled=True)[0]
    chosen = lax.dynamic_slice_in_dim(plan[0], own * per_device, per_device)
    query_rows = (chosen[:, None] * BLOCK + jnp.arange(BLOCK, dtype=jnp.int32)[None, :]).reshape(-1)
    query_tensor = jnp.take(all_queries, query_rows, axis=0).reshape(
        local, kv_count, query_group, HEAD_SIZE
    )
    query_doc = jnp.take(doc_of, query_rows)

    def allowed_for(count):
        key_rows = jnp.arange(count, dtype=jnp.int32)
        return (key_rows[None, :] <= query_rows[:, None]) & (doc_of[None, :] == query_doc[:, None])

    opening = (
        jnp.full((kv_count, query_group, local), NEG_FILL, jnp.float32),
        jnp.zeros((kv_count, query_group, local), jnp.float32),
        jnp.zeros((kv_count, query_group, local, HEAD_SIZE), jnp.float32),
    )
    pieces = (
        lax.all_gather(k_in, "seq", axis=1, tiled=True),
        lax.all_gather(value_input, "seq", axis=1, tiled=True),
    )
    key_tensor = pieces[0][0].reshape(-1, kv_count, HEAD_SIZE)
    value_tensor = pieces[1][0].reshape(-1, kv_count, HEAD_SIZE)
    mask = allowed_for(key_tensor.shape[0])

    def forward_update(state):
        run_max, run_sum, run_acc = state
        scores = (
            jnp.einsum(
                "qhgd,khd->hgqk", query_tensor, key_tensor, preferred_element_type=jnp.float32
            )
            * scale
        )
        new_max = jnp.maximum(run_max, jnp.max(jnp.where(mask, scores, NEG_FILL), axis=-1))
        weights = jnp.where(mask, jnp.exp(scores - new_max[..., None]), 0.0)
        new_sum = jnp.sum(weights, axis=-1)
        added = jnp.einsum(
            "hgqk,khd->hgqd",
            weights.astype(jnp.bfloat16),
            value_tensor,
            preferred_element_type=jnp.float32,
        )
        return (new_max, new_sum, added)

    run_max, run_sum, run_acc = lax.cond(jnp.any(mask), forward_update, keep_state, opening)
    lse = run_max + jnp.log(run_sum)
    attended_output = jnp.transpose(
        (run_acc / run_sum[..., None]).astype(jnp.bfloat16), (2, 0, 1, 3)
    )
    attn_out = attended_output.reshape(local, head_count * HEAD_SIZE)
    d_att = dout_in[0].reshape(local, kv_count, query_group, HEAD_SIZE)
    rowdot = jnp.transpose(
        jnp.sum(d_att.astype(jnp.float32) * attended_output.astype(jnp.float32), axis=-1), (1, 2, 0)
    )
    query_zero = jnp.zeros((kv_count, query_group, local, HEAD_SIZE), jnp.float32)
    initial = (
        query_zero,
        jnp.zeros((row_tokens, kv_count * HEAD_SIZE), jnp.float32),
        jnp.zeros((row_tokens, kv_count * HEAD_SIZE), jnp.float32),
    )
    pieces = (
        lax.all_gather(k_in, "seq", axis=1, tiled=True),
        lax.all_gather(value_input, "seq", axis=1, tiled=True),
    )
    start = jnp.int32(0)
    backward_key_tensor = pieces[0][0].reshape(-1, kv_count, HEAD_SIZE)
    backward_value_tensor = pieces[1][0].reshape(-1, kv_count, HEAD_SIZE)
    count = backward_key_tensor.shape[0]
    backward_mask = allowed_for(count)

    def backward_update(state):
        query_part, key_part, value_part = piece_grads(
            query_tensor,
            d_att,
            lse,
            rowdot,
            backward_key_tensor,
            backward_value_tensor,
            backward_mask,
            scale,
        )
        key_old = state[1]
        value_old = state[2]
        return (
            state[0] + query_part,
            lax.dynamic_update_slice_in_dim(state[1], key_old + key_part, start, 0),
            lax.dynamic_update_slice_in_dim(state[2], value_old + value_part, start, 0),
        )

    query_acc, key_all, value_all = lax.cond(
        jnp.any(backward_mask), backward_update, keep_state, initial
    )
    key_sum, value_sum = (
        lax.psum_scatter(key_all[None], "seq", scatter_dimension=1, tiled=True),
        lax.psum_scatter(value_all[None], "seq", scatter_dimension=1, tiled=True),
    )
    key_gradient = key_sum.astype(jnp.bfloat16)
    value_gradient = value_sum.astype(jnp.bfloat16)
    query_gradient = (
        jnp.transpose(query_acc, (2, 0, 1, 3))
        .reshape(local, head_count * HEAD_SIZE)
        .astype(jnp.bfloat16)
    )
    return (
        output_all[None],
        input_all[None],
        raw_all[None],
        b_sum.T[None],
        c_sum.T[None],
        rate_sum,
        skip_sum,
        bias_sum,
        attn_out[None],
        query_gradient[None],
        key_gradient,
        value_gradient,
    )


def solution(mesh):
    in_specs = (
        P("dp", "seq", "tp"),
        P("dp", "seq", "tp"),
        P("dp", None, "seq"),
        P("dp", None, "seq"),
        P("dp", "seq", "tp"),
        P(None, "tp"),
        P("tp"),
        P("tp"),
        P("dp", "seq", "tp"),
        P("dp", "seq", "tp"),
        P("dp", "seq", "tp"),
        P("dp", "seq", "tp"),
        P("dp", None),
        P("dp", None),
    )
    out_specs = (
        P("dp", "seq", "tp"),
        P("dp", "seq", "tp"),
        P("dp", "seq", "tp"),
        P("dp", None, "seq"),
        P("dp", None, "seq"),
        P(None, "tp"),
        P("tp"),
        P("tp"),
        P("dp", "seq", "tp"),
        P("dp", "seq", "tp"),
        P("dp", "seq", "tp"),
        P("dp", "seq", "tp"),
    )
    return jax.shard_map(
        on_device, mesh=mesh, in_specs=in_specs, out_specs=out_specs, check_vma=False
    )
```

profile of v0, /device:TPU:4, one launch (start us, length us, event | category | flops | bytes accessed | tf_op | source)
XLA Modules:
  0.0 917.2 jit_solution(15452079686889604294)
XLA Ops:
  16.7 231.0 %while.72 = (s32[]{:T(128)}, f32[4,16,128]{2,1,0:T(8,128)}, f32[4,16,128]{2,1,0:T(8,128)}, f32[4,16,128]{2,1,0:T(8,128)}, f32[4,16,128]{2,1,0:T(8,128)}, /*index...) while((s32[]{:T(128)}, f32[4,16,128]{2,1,0:T(8,128)}, ...), condition=%wide.region_3.4_spmd, body=%wide.region_2.3_spmd.sunk | while | flops 6914053 | bytes 49321408 | solution.py:157
  36.2 1.9 pad.606
  38.1 1.9 pad.605
  40.0 1.9 pad.607
  43.2 1.9 pad.608
  50.6 3.2 pad.609
  55.2 3.2 pad.611
  58.4 3.2 pad.610
  63.1 3.2 pad.612
  93.9 1.9 pad.606
  95.8 1.9 pad.605
  101.0 1.9 pad.608
  108.4 3.2 pad.609
  112.9 3.2 pad.611
  116.1 3.2 pad.610
  120.9 3.2 pad.612
  151.7 1.9 pad.606
  153.6 1.9 pad.605
  158.7 1.9 pad.608
  166.1 3.2 pad.609
  170.7 3.2 pad.611
  173.9 3.2 pad.610
  178.6 3.2 pad.612
  209.4 1.9 pad.606
  211.3 1.9 pad.605
  216.4 1.9 pad.608
  223.9 3.2 pad.609
  228.4 3.2 pad.611
  231.6 3.2 pad.610
  236.3 3.2 pad.612
  250.9 38.5 %all_gather.25 = f32[16,16,512]{2,1,0:T(8,128)S(1)} all-gather(f32[1,16,512]{2,1,0:T(8,128)S(1)} %all_gather_reshape.14), channel_id=1, replica_groups=mesh['seq'=16,'tp'=8,'dp'=4] {'seq'}, dimensions={0}, use_global_device_ids=true | all-gather | bytes 557056 | tf_op jit(solution)/shard_map/all_gather | solution.py:18
  289.4 29.2 %all_gather.24 = f32[16,16,512]{2,1,0:T(8,128)S(1)} all-gather(f32[1,16,512]{2,1,0:T(8,128)S(1)} %all_gather_reshape.13), channel_id=1, replica_groups=mesh['seq'=16,'tp'=8,'dp'=4] {'seq'}, dimensions={0}, use_global_device_ids=true | all-gather | bytes 557056 | tf_op jit(solution)/shard_map/all_gather | solution.py:18
  318.6 31.3 %all_gather.23 = f32[16,16,512]{2,1,0:T(8,128)S(1)} all-gather(f32[1,16,512]{2,1,0:T(8,128)S(1)} %all_gather_reshape.12), channel_id=1, replica_groups=mesh['seq'=16,'tp'=8,'dp'=4] {'seq'}, dimensions={0}, use_global_device_ids=true | all-gather | bytes 557056 | tf_op jit(solution)/shard_map/all_gather | solution.py:18
  349.8 29.0 %all_gather.26 = f32[16,16,512]{2,1,0:T(8,128)S(1)} all-gather(f32[1,16,512]{2,1,0:T(8,128)S(1)} %all_gather_reshape.15), channel_id=1, replica_groups=mesh['seq'=16,'tp'=8,'dp'=4] {'seq'}, dimensions={0}, use_global_device_ids=true | all-gather | bytes 557056 | tf_op jit(solution)/shard_map/all_gather | solution.py:18
  385.9 31.1 %all_gather.27 = bf16[1,2048,128]{2,1,0:T(8,128)(2,1)S(1)} all-gather(bf16[1,128,128]{2,1,0:T(8,128)(2,1)S(1)} %copy-done.24), channel_id=1, replica_groups=mesh['seq'=16,'tp'=8,'dp'=4] {'seq'}, dimensions={1}, use_global_device_ids=true | all-gather | bytes 557056 | tf_op jit(solution)/shard_map/all_gather | solution.py:246
  417.0 28.7 %all_gather.29 = bf16[1,2048,128]{2,1,0:T(8,128)(2,1)S(1)} all-gather(bf16[1,128,128]{2,1,0:T(8,128)(2,1)S(1)} %copy-done.25), channel_id=1, replica_groups=mesh['seq'=16,'tp'=8,'dp'=4] {'seq'}, dimensions={1}, use_global_device_ids=true | all-gather | bytes 557056 | tf_op jit(solution)/shard_map/all_gather | solution.py:247
  445.7 20.0 %while.73 = (s32[]{:T(128)}, f32[16,512]{1,0:T(8,128)}, s32[]{:T(128)}, f32[16,16,512]{2,1,0:T(8,128)S(1)}, f32[16,16,512]{2,1,0:T(8,128)S(1)}, /*index=5*/s32[]{:T(128)}, s32[]{:T(128)}) while((s32[]{:T(128)}, f32[16,512]{1,0:T(8,128)}, s32[]{:T(128)}, f32[16,16,512]{2,1,0:T(8,128)S(1)}, f32[16,16,512]{2,1,0:T(8,128)S(1)}, ...), condition=%wide.region_5.6_spmd.clone, body=%wide.region_4.5_spmd.clone.sunk | while | flops 32772 | bytes 131181 | solution.py:30
  465.7 2.9 gather_fusion.1
  468.7 2.6 conditional.2
  472.0 5.7 conditional.3
  478.7 21.2 %while.74 = (s32[]{:T(128)}, f32[16,512]{1,0:T(8,128)}, s32[]{:T(128)}, f32[16,16,512]{2,1,0:T(8,128)}, f32[16,16,512]{2,1,0:T(8,128)}, /*index=5*/s32[]{:T(128)}, s32[]{:T(128)}) while((s32[]{:T(128)}, f32[16,512]{1,0:T(8,128)}, s32[]{:T(128)}, f32[16,16,512]{2,1,0:T(8,128)}, f32[16,16,512]{2,1,0:T(8,128)}, /*index=5*/s32[]{:T(128)}, ...), condition=%wide.region_7.8_spmd.clone, body=%wide.region_6.7_spmd.clone.sunk | while | flops 32772 | bytes 131181 | solution.py:30
  503.2 101.4 %while.75 = (s32[]{:T(128)}, bf16[128,512]{1,0:T(8,128)(2,1)}, bf16[128,512]{1,0:T(8,128)(2,1)}, bf16[128,512]{1,0:T(8,128)(2,1)}, f32[128,16]{1,0:T(8,128)}, /*...) while((s32[]{:T(128)}, bf16[128,512]{1,0:T(8,128)(2,1)}, ...), condition=%wide.region_17.18_spmd.clone, body=%wide.region_8.17_spmd.clone.sunk | while | flops 14495493 | bytes 66015552 | solution.py:218
  522.2 2.1 multiply_reduce_fusion.13
  547.5 2.1 multiply_reduce_fusion.13
  572.9 2.1 multiply_reduce_fusion.13
  598.3 2.1 multiply_reduce_fusion.13
  605.6 25.0 %all-reduce.59 = (f32[1,16,128]{2,1,0:T(8,128)}, f32[1,16,128]{2,1,0:T(8,128)}) all-reduce(f32[1,16,128]{2,1,0:T(8,128)S(1)} %bitcast.1836, f32[1,16,128]{2,1,0:T(8,128)S(1)} %bitcast.1837), channel_id=1, replica_groups=mesh['seq'=16,'tp'=8,'dp'=4] {'tp'}, use_global_device_ids=true, to_apply=%region_18.19 | all-reduce | flops 4096 | bytes 32768 | tf_op jit(solution)/shard_map/psum | solution.py:221
  630.6 273.7 %all-reduce.58 = (f32[16,512]{1,0:T(8,128)}, f32[512]{0:T(512)}, f32[512]{0:T(512)}) all-reduce(f32[16,512]{1,0:T(8,128)} %get-tuple-element.656, f32[512]{0:T(512)S(1)} %get-tuple-element.657, f32[512]{0:T(512)} %get-tuple-element.658), channel_id=1, replica_groups=mesh['seq'=16,'tp'=8,'dp'=4] {'seq','dp'}, use_global_device_ids=true, to_apply=%region_20.21 | all-reduce | flops 9216 | bytes 73728 | tf_op jit(solution)/shard_map/psum | solution.py:222
  (1337 shorter events, 319.0 us)
Async XLA Ops:
  7.2 458.5 %all-gather.2.cloned.1.call-start = ((), (), s32[]{:S(2)}) async-start(), calls=%async_computation.2 | async-start | bytes 2228224 | tf_op jit(solution)/shard_map/all_gather | solution.py:228
  7.9 899.8 %reduce-scatter.3.cloned.1.call-start = ((), (), s32[]{:S(2)}) async-start(), calls=%async_computation.3 | async-start | bytes 1114112 | tf_op jit(solution)/shard_map/reduce_scatter | solution.py:321
  31.7 2.0 copy-start.2
  66.3 7.3 copy-start.7
  89.5 2.0 copy-start.2
  124.1 7.3 copy-start.7
  147.2 2.0 copy-start.2
  181.8 7.3 copy-start.7
  239.5 7.3 copy-start.7
  247.6 138.2 %copy-start.24 = (bf16[1,128,128]{2,1,0:T(8,128)(2,1)S(1)}, bf16[1,128,128]{2,1,0:T(8,128)(2,1)}, u32[]{:S(2)}) copy-start(bf16[1,128,128]{2,1,0:T(8,128)(2,1)} %param.35) | copy-start | bytes 98308
  247.7 169.3 %copy-start.25 = (bf16[1,128,128]{2,1,0:T(8,128)(2,1)S(1)}, bf16[1,128,128]{2,1,0:T(8,128)(2,1)}, u32[]{:S(2)}) copy-start(bf16[1,128,128]{2,1,0:T(8,128)(2,1)} %param.36) | copy-start | bytes 98308
  472.0 31.2 %copy-start.4 = (f32[128,16]{1,0:T(8,128)S(1)}, f32[128,16]{1,0:T(8,128)}, u32[]{:S(2)}) copy-start(f32[128,16]{1,0:T(8,128)} %copy-done.3) | copy-start | bytes 24580
  472.0 31.2 %copy-start.5 = (bf16[1,128,512]{2,1,0:T(8,128)(2,1)S(1)}, bf16[1,128,512]{2,1,0:T(8,128)(2,1)}, u32[]{:S(2)}) copy-start(bf16[1,128,512]{2,1,0:T(8,128)(2,1)} %get-tuple-element.2109) | copy-start | bytes 393220
  474.8 2.1 copy-start.18
  477.7 22.3 %copy-start.9 = (f32[2048,128]{1,0:T(8,128)}, f32[2048,128]{1,0:T(8,128)S(1)}, u32[]{:S(2)}) copy-start(f32[2048,128]{1,0:T(8,128)S(1)} %get-tuple-element.664) | copy-start | bytes 3145732
  478.7 430.5 %reduce-scatter.5.cloned.1.call-start = ((), (), s32[]{:S(2)}) async-start(), calls=%async_computation.4 | async-start | bytes 1114112 | tf_op jit(solution)/shard_map/reduce_scatter | solution.py:322
  504.0 11.9 %copy-start.20 = (f32[128]{0:T(128)}, f32[128]{0:T(128)S(1)}, u32[]{:S(2)}) copy-start(f32[128]{0:T(128)S(1)} %dynamic_slice.213) | copy-start | bytes 1540 | tf_op jit(solution)/shard_map/while
  504.7 11.1 %copy-start.22 = (f32[128]{0:T(128)}, f32[128]{0:T(128)S(1)}, u32[]{:S(2)}) copy-start(f32[128]{0:T(128)S(1)} %dynamic_slice.212) | copy-start | bytes 1540 | tf_op jit(solution)/shard_map/while
  513.8 4.4 copy-start.8
  521.2 3.1 copy-start.21
  521.2 5.8 copy-start.13
  521.2 5.8 copy-start.23
  521.2 7.3 copy-start.12
  521.2 7.3 copy-start.27
  529.3 11.9 %copy-start.20 = (f32[128]{0:T(128)}, f32[128]{0:T(128)S(1)}, u32[]{:S(2)}) copy-start(f32[128]{0:T(128)S(1)} %dynamic_slice.213) | copy-start | bytes 1540 | tf_op jit(solution)/shard_map/while
  530.1 11.1 %copy-start.22 = (f32[128]{0:T(128)}, f32[128]{0:T(128)S(1)}, u32[]{:S(2)}) copy-start(f32[128]{0:T(128)S(1)} %dynamic_slice.212) | copy-start | bytes 1540 | tf_op jit(solution)/shard_map/while
  539.1 4.4 copy-start.8
  546.6 3.1 copy-start.21
  546.6 5.8 copy-start.13
  546.6 5.8 copy-start.23
  546.6 7.3 copy-start.12
  546.6 7.3 copy-start.27
  554.7 11.9 %copy-start.20 = (f32[128]{0:T(128)}, f32[128]{0:T(128)S(1)}, u32[]{:S(2)}) copy-start(f32[128]{0:T(128)S(1)} %dynamic_slice.213) | copy-start | bytes 1540 | tf_op jit(solution)/shard_map/while
  555.4 11.1 %copy-start.22 = (f32[128]{0:T(128)}, f32[128]{0:T(128)S(1)}, u32[]{:S(2)}) copy-start(f32[128]{0:T(128)S(1)} %dynamic_slice.212) | copy-start | bytes 1540 | tf_op jit(solution)/shard_map/while
  564.5 4.4 copy-start.8
  571.9 3.1 copy-start.21
  571.9 5.8 copy-start.13
  571.9 5.8 copy-start.23
  572.0 7.3 copy-start.12
  572.0 7.3 copy-start.27
  580.0 11.9 %copy-start.20 = (f32[128]{0:T(128)}, f32[128]{0:T(128)S(1)}, u32[]{:S(2)}) copy-start(f32[128]{0:T(128)S(1)} %dynamic_slice.213) | copy-start | bytes 1540 | tf_op jit(solution)/shard_map/while
  580.8 11.1 %copy-start.22 = (f32[128]{0:T(128)}, f32[128]{0:T(128)S(1)}, u32[]{:S(2)}) copy-start(f32[128]{0:T(128)S(1)} %dynamic_slice.212) | copy-start | bytes 1540 | tf_op jit(solution)/shard_map/while
  589.8 4.4 copy-start.8
  597.3 3.1 copy-start.21
  597.3 5.8 copy-start.13
  597.3 5.8 copy-start.23
  597.3 7.3 copy-start.12
  597.3 7.3 copy-start.27
  (34 other events, 37.5 us)
Sparse Core Ops, SparseCore 0:
  10.1 77.5 all-gather.1
  478.8 66.7 reduce-scatter.2
  548.6 68.2 reduce-scatter.4
where the time goes:
time: 931 us; the launch traced here: 917 us
  blocking collectives  487 us (52%)
  local copies, waits for them, and re-layouts  202 us (22%)
  other arithmetic  198 us (21%)
  between operations  14.6 us (2%)
  loops' own time  9.68 us (1%)
    psum x1, blocking collectives, on_device(): lax.psum((rate_all, skip_all, bias_all), ('seq', 'dp'))  274 us
    all_gather x4, blocking collectives, carried_in(): pieces = jax.tree.map(lambda part: lax.all_gather(part, axis), value)  128 us
    while x324, local copies, waits for them, and re-layouts  46.6 us
    select_n x30, other arithmetic, turn(): jnp.where(position < mine, new, old)  41.2 us
    pad x64, local copies, waits for them, and re-layouts, block_scan(): lax.associative_scan(pair_combine, (factor_in[:, -1], state_in[:, -1]))  31.5 us
    all_gather x1, blocking collectives, on_device(): lax.all_gather(k_in, 'seq', axis=1, tiled=True)  31.1 us
    all_gather x1, blocking collectives, on_device(): lax.all_gather(value_input, 'seq', axis=1, tiled=True)  28.7 us
    psum x1, blocking collectives, on_device(): b_sum, c_sum = lax.psum((b_total, c_total), 'tp')  25 us
  transfers between devices with their start and end apart: 3, of which 0 were waited for; matrix products, arithmetic and copies ran while one was open for 42% of the time, Pallas kernels for 0%

commit v1 on v0

v1 whole, which is shorter than its diff:
```python
import functools

import jax
import jax.numpy as jnp
from jax import lax
from jax.experimental import pallas as pl
from jax.experimental.pallas import tpu as pltpu
from jax.sharding import PartitionSpec as P

NS = 16
HEAD = 128
BLOCK = 32
LANES = 128
SEGS = 8
RESET = 1e30
LOG2E = 1.4426950408889634
NEG = -1e30
KEYS = 256
SUMMARY_ROWS = 48

F32 = jnp.float32
BF16 = jnp.bfloat16


def dot(a, b, dims=((1,), (0,)), precision=None):
    return lax.dot_general(a, b, (dims, ((), ())), precision=precision, preferred_element_type=F32)


def exact_dot(a, b, dims=((1,), (0,))):
    return dot(a, b, dims, lax.Precision.HIGHEST)


def iota(shape, axis):
    return lax.broadcasted_iota(jnp.int32, shape, axis)


def to_segments(tokens):
    span = tokens // SEGS
    row = iota((tokens, tokens), 0)
    token = iota((tokens, tokens), 1)
    return jnp.where(token == lax.rem(row, SEGS) * span + lax.div(row, SEGS), 1.0, 0.0)


def to_tokens(tokens):
    span = tokens // SEGS
    token = iota((tokens, tokens), 0)
    row = iota((tokens, tokens), 1)
    return jnp.where(row == lax.rem(token, span) * SEGS + lax.div(token, span), 1.0, 0.0)


def starts_of(lengths_ref):
    starts = [jnp.int32(0)]
    for k in range(lengths_ref.shape[0] - 1):
        starts.append(starts[-1] + lengths_ref[k])
    return starts


def softplus_of(raw):
    small = jnp.exp(-jnp.abs(raw))
    one = 1.0 + small
    tail = one - 1.0
    safe = jnp.where(tail == 0.0, 1.0, tail)
    log1p = jnp.where(tail == 0.0, small, jnp.log(one) * (small / safe))
    return jnp.maximum(raw, 0.0) + log1p


def step_sizes(own_ref, lengths_ref, segment, dt_ref, bias_ref, tokens):
    raw = dot(segment, dt_ref[...]) + bias_ref[...]
    delta = softplus_of(raw)
    span = tokens // SEGS
    row = iota(delta.shape, 0)
    token = own_ref[0] * tokens + lax.rem(row, SEGS) * span + lax.div(row, SEGS)
    first = token == 0
    for start in starts_of(lengths_ref):
        first = first | (token == start)
    return raw, delta, jnp.where(first, RESET, delta)


def spread(source, target):
    for n in range(NS):
        target[n] = jnp.broadcast_to(source[n : n + 1], target.shape[1:])


def fill_columns(segment, b_ref, c_ref, b_wide, c_wide):
    tokens = segment.shape[0]
    for source, target in ((b_ref, b_wide), (c_ref, c_wide)):
        columns = dot(segment, source[...], ((1,), (1,)))
        for n in range(NS):
            target[n] = jnp.broadcast_to(columns[:, n : n + 1], (tokens, LANES))


def shifted(value, by, fill):
    rows = value.shape[0]
    row = iota(value.shape, 0)
    moved = pltpu.roll(value, by % rows, 0)
    return jnp.where((row >= by) & (row < rows + by), moved, fill)


def summary_kernel(
    own_ref, lengths_ref, x_ref, dt_ref, dy_ref, b_ref, c_ref, a_ref, bias_ref,
    summary_ref, seg_state_ref, seg_adjoint_ref, seg_delta_ref,
    rate2_ref, b_wide, c_wide, decay_delta, drive, upstream, before_ref, after_ref,
):
    tokens, width = x_ref.shape
    span = tokens // SEGS
    segment = to_segments(tokens).astype(BF16)
    spread(-jnp.exp(a_ref[...]) * LOG2E, rate2_ref)
    raw, delta, reset_delta = step_sizes(own_ref, lengths_ref, segment, dt_ref, bias_ref, tokens)
    decay_delta[...] = reset_delta
    drive[...] = delta * dot(segment, x_ref[...])
    upstream[...] = dot(segment, dy_ref[...])
    fill_columns(segment, b_ref, c_ref, b_wide, c_wide)

    total = reset_delta[:SEGS]
    for pos in range(1, span):
        total = total + reset_delta[pos * SEGS : (pos + 1) * SEGS]
    seg_delta_ref[...] = total
    after = shifted(total, -1, 0.0)
    before = shifted(total, 1, 0.0)
    for by in (1, 2, 4):
        after = after + shifted(after, -by, 0.0)
        before = before + shifted(before, by, 0.0)
    after_ref[...] = after
    before_ref[...] = before
    whole = before[SEGS - 1 :] + total[SEGS - 1 :]
    high = whole.astype(BF16)
    low = (whole - high.astype(F32)).astype(BF16)
    summary_ref[2 * NS :] = jnp.zeros((SUMMARY_ROWS - 2 * NS, width), BF16)
    summary_ref[2 * NS : 2 * NS + 1] = high
    summary_ref[2 * NS + 1 : 2 * NS + 2] = low

    def state_row(n, carry):
        state_rows, adjoint_rows = [], []
        for lane in range(0, width, LANES):
            cols = slice(lane, lane + LANES)
            rate2 = rate2_ref[n, :, cols]
            state = jnp.zeros((SEGS, LANES), F32)
            decays = []
            for pos in range(span):
                rows = slice(pos * SEGS, (pos + 1) * SEGS)
                decay = jnp.exp2(rate2 * decay_delta[rows, cols])
                decays.append(decay)
                state = decay * state + b_wide[n, rows] * drive[rows, cols]
            adjoint = jnp.zeros((SEGS, LANES), F32)
            for pos in reversed(range(span)):
                rows = slice(pos * SEGS, (pos + 1) * SEGS)
                adjoint = decays[pos] * (c_wide[n, rows] * upstream[rows, cols] + adjoint)
            seg_state_ref[n, :, cols] = state
            seg_adjoint_ref[n, :, cols] = adjoint
            weight = jnp.exp2(rate2 * after_ref[:, cols])
            state_rows.append(jnp.sum(weight * state, axis=0, keepdims=True))
            weight = jnp.exp2(rate2 * before_ref[:, cols])
            adjoint_rows.append(jnp.sum(weight * adjoint, axis=0, keepdims=True))
        sel = iota((NS, width), 0) == n
        states, adjoints = carry
        states = jnp.where(sel, jnp.concatenate(state_rows, 1), states)
        adjoints = jnp.where(sel, jnp.concatenate(adjoint_rows, 1), adjoints)
        return states, adjoints

    zero = jnp.zeros((NS, width), F32)
    states, adjoints = lax.fori_loop(0, NS, state_row, (zero, zero))
    summary_ref[:NS] = states.astype(BF16)
    summary_ref[NS : 2 * NS] = adjoints.astype(BF16)


def mixer_kernel(
    own_ref, lengths_ref, x_ref, dt_ref, dy_ref, b_ref, c_ref, a_ref, bias_ref, skip_ref,
    summaries_ref, seg_state_ref, seg_adjoint_ref, seg_delta_ref,
    out_ref, x_grad_ref, dt_grad_ref, bc_ref, params_ref,
    rate_ref, rate2_ref, b_wide, c_wide, delta_ref, decay_delta, drive, upstream,
    enter_ref, arrive_ref, y_acc, xg_acc, dd_acc, bg_acc, cg_acc, rate_acc,
):
    tokens, width = x_ref.shape
    span = tokens // SEGS
    count = summaries_ref.shape[0]
    own = own_ref[0]
    segment = to_segments(tokens).astype(BF16)
    rate_all = -jnp.exp(a_ref[...])
    rate2_all = rate_all * LOG2E
    spread(rate_all, rate_ref)
    spread(rate2_all, rate2_ref)
    raw, delta, reset_delta = step_sizes(own_ref, lengths_ref, segment, dt_ref, bias_ref, tokens)
    delta_ref[...] = delta
    decay_delta[...] = reset_delta
    inputs = dot(segment, x_ref[...])
    drive[...] = delta * inputs
    upstream[...] = dot(segment, dy_ref[...])
    fill_columns(segment, b_ref, c_ref, b_wide, c_wide)

    entering = jnp.zeros((NS, width), F32)
    arriving = jnp.zeros((NS, width), F32)

    def factor(j):
        ends = summaries_ref[j, 2 * NS : 2 * NS + 2].astype(F32)
        return jnp.exp2(rate2_all * (ends[0:1] + ends[1:2]))

    for j in range(count - 1):
        longer = factor(j) * entering + summaries_ref[j, :NS].astype(F32)
        entering = jnp.where(j < own, longer, entering)
    for j in reversed(range(1, count)):
        longer = factor(j) * arriving + summaries_ref[j, NS : 2 * NS].astype(F32)
        arriving = jnp.where(j > own, longer, arriving)
    spread(entering, enter_ref)
    spread(arriving, arrive_ref)

    y_acc[...] = jnp.zeros_like(y_acc)
    xg_acc[...] = jnp.zeros_like(xg_acc)
    dd_acc[...] = jnp.zeros_like(dd_acc)

    def state_row(n, carry):
        for lane in range(0, width, LANES):
            cols = slice(lane, lane + LANES)
            rate = rate_ref[n, :, cols]
            rate2 = rate2_ref[n, :, cols]
            row = iota((SEGS, LANES), 0)
            seg_factor = jnp.exp2(rate2 * seg_delta_ref[:, cols])
            edge = enter_ref[n, :, cols]
            scale, total = seg_factor, seg_state_ref[n, :, cols]
            for by in (1, 2, 4):
                total = total + scale * shifted(total, by, 0.0)
                scale = scale * shifted(scale, by, 1.0)
            state = jnp.where(row == 0, edge, pltpu.roll(total + scale * edge, 1, 0))
            edge = arrive_ref[n, :, cols]
            scale, total = seg_factor, seg_adjoint_ref[n, :, cols]
            for by in (1, 2, 4):
                total = total + scale * shifted(total, -by, 0.0)
                scale = scale * shifted(scale, -by, 1.0)
            moved = pltpu.roll(total + scale * edge, SEGS - 1, 0)
            adjoint = jnp.where(row == SEGS - 1, edge, moved)
            decays, befores = [], []
            for pos in range(span):
                rows = slice(pos * SEGS, (pos + 1) * SEGS)
                decay = jnp.exp2(rate2 * decay_delta[rows, cols])
                decays.append(decay)
                befores.append(state)
                state = decay * state + b_wide[n, rows] * drive[rows, cols]
                y_acc[rows, cols] += c_wide[n, rows] * state
                part = upstream[rows, cols] * state
                if lane == 0:
                    cg_acc[n, rows] = part
                else:
                    cg_acc[n, rows] += part
            rate_sum = jnp.zeros((SEGS, LANES), F32)
            for pos in reversed(range(span)):
                rows = slice(pos * SEGS, (pos + 1) * SEGS)
                full = c_wide[n, rows] * upstream[rows, cols] + adjoint
                adjoint = decays[pos] * full
                xg_acc[rows, cols] += full * b_wide[n, rows]
                part = full * drive[rows, cols]
                if lane == 0:
                    bg_acc[n, rows] = part
                else:
                    bg_acc[n, rows] += part
                through = adjoint * befores[pos]
                dd_acc[rows, cols] += rate * through
                rate_sum = rate_sum + delta_ref[rows, cols] * through
            rate_acc[n, :, cols] = rate * rate_sum
        return carry

    lax.fori_loop(0, NS, state_row, 0)

    token = to_tokens(tokens).astype(BF16)
    inputs = dot(segment, x_ref[...])
    skip = skip_ref[...]
    out_ref[...] = dot(token, (y_acc[...] + skip * inputs).astype(BF16)).astype(BF16)
    x_grad = xg_acc[...] * delta_ref[...] + skip * upstream[...]
    x_grad_ref[...] = dot(token, x_grad.astype(BF16)).astype(BF16)
    raw = dot(segment, dt_ref[...]) + bias_ref[...]
    raw_grad = (xg_acc[...] * inputs + dd_acc[...]) / (1.0 + jnp.exp(-raw))
    dt_grad_ref[...] = dot(token, raw_grad.astype(BF16)).astype(BF16)
    params_ref[:NS] = jnp.sum(rate_acc[...], axis=1)
    params_ref[NS : NS + 1] = jnp.sum(upstream[...] * inputs, axis=0, keepdims=True)
    params_ref[NS + 1 : NS + 2] = jnp.sum(raw_grad, axis=0, keepdims=True)
    ones = jnp.ones((SEGS, LANES), F32)
    sums = []
    for source in (bg_acc, cg_acc):
        for n in range(NS):
            sums.append(exact_dot(ones, source[n], ((1,), (1,)))[:1])
    bc_ref[...] = exact_dot(jnp.concatenate(sums, 0), to_segments(tokens))


def attention_kernel(
    own_ref, lengths_ref, plan_ref, all_ref, dout_ref,
    out_ref, query_grad_ref, kv_grad_ref,
    query_t, dout_t, score_ref, turned, out_acc, query_acc,
):
    tokens, width = dout_ref.shape
    rows_all = all_ref.shape[0]
    heads = width // HEAD
    columns = heads * tokens
    places = tokens // BLOCK
    factor = (HEAD ** -0.5) * LOG2E
    starts = starts_of(lengths_ref)
    wanted = [plan_ref[own_ref[0] * places + p] for p in range(places)]

    picked = jnp.concatenate(
        [all_ref[pl.ds(pl.multiple_of(w * BLOCK, BLOCK), BLOCK), :width] for w in wanted], 0
    )
    dout = dout_ref[...]
    query = jnp.concatenate([picked[:, h * HEAD : (h + 1) * HEAD] for h in range(heads)], 0)
    d_att = jnp.concatenate([dout[:, h * HEAD : (h + 1) * HEAD] for h in range(heads)], 0)
    query_t[...] = query.astype(F32).T.astype(BF16)
    dout_t[...] = d_att.astype(F32).T.astype(BF16)

    column = lax.rem(iota((1, columns), 1), tokens)
    place = lax.div(column, BLOCK)
    block = jnp.zeros((1, columns), jnp.int32)
    for p, w in enumerate(wanted):
        block = jnp.where(place == p, w, block)
    last = block * BLOCK + lax.rem(column, BLOCK)
    opening = jnp.zeros((1, columns), jnp.int32)
    for start in starts:
        opening = jnp.where(start <= last, start, opening)

    lowest = jnp.int32(rows_all)
    highest = jnp.int32(0)
    for w in wanted:
        low = jnp.int32(0)
        for start in starts:
            low = jnp.where(start <= w * BLOCK, start, low)
        lowest = jnp.minimum(lowest, low)
        highest = jnp.maximum(highest, w * BLOCK + BLOCK)
    begin = lax.div(lowest, KEYS)
    end = lax.div(highest + KEYS - 1, KEYS)

    def at(j):
        return pl.ds(pl.multiple_of(j * KEYS, KEYS), KEYS)

    def score_step(j, top):
        scores = dot(all_ref[at(j), width : width + HEAD], query_t[...])
        key = j * KEYS + iota((KEYS, columns), 0)
        scores = jnp.where((key <= last) & (key >= opening), scores, NEG)
        score_ref[at(j)] = scores
        return jnp.maximum(top, jnp.max(scores.reshape(KEYS // 8, 8, columns), axis=0))

    top = lax.fori_loop(begin, end, score_step, jnp.full((8, columns), NEG, F32))
    shift = jnp.max(top, axis=0, keepdims=True) * factor

    out_acc[...] = jnp.zeros_like(out_acc)

    def weight_step(j, total):
        weights = jnp.exp2(score_ref[at(j)] * factor - shift)
        score_ref[at(j)] = weights
        value_t = all_ref[at(j), width + HEAD :].astype(F32).T.astype(BF16)
        out_acc[...] += dot(value_t, weights.astype(BF16))
        return total + jnp.sum(weights.reshape(KEYS // 8, 8, columns), axis=0)

    total = lax.fori_loop(begin, end, weight_step, jnp.zeros((8, columns), F32))
    inverse = 1.0 / jnp.sum(total, axis=0, keepdims=True)
    attended = (out_acc[...] * inverse).astype(BF16)
    rowdot = jnp.sum(attended.astype(F32) * dout_t[...].astype(F32), axis=0, keepdims=True)
    turned[...] = attended.astype(F32).T
    for h in range(heads):
        out_ref[:, h * HEAD : (h + 1) * HEAD] = turned[h * tokens : (h + 1) * tokens].astype(BF16)

    query_acc[...] = jnp.zeros_like(query_acc)
    kv_grad_ref[...] = jnp.zeros_like(kv_grad_ref)

    def gradient_step(j, carry):
        keys = all_ref[at(j), width : width + HEAD]
        d_probs = dot(all_ref[at(j), width + HEAD :], dout_t[...])
        probs = score_ref[at(j)] * inverse
        d_scores = (probs * (d_probs - rowdot)).astype(BF16)
        query_acc[...] += dot(keys.astype(F32).T.astype(BF16), d_scores)
        key_grad = dot(d_scores, query) * (HEAD ** -0.5)
        value_grad = dot(probs.astype(BF16), d_att)
        kv_grad_ref[at(j), :HEAD] = key_grad.astype(BF16)
        kv_grad_ref[at(j), HEAD:] = value_grad.astype(BF16)
        return carry

    lax.fori_loop(begin, end, gradient_step, 0)
    turned[...] = (query_acc[...] * (HEAD ** -0.5)).T
    for h in range(heads):
        query_grad_ref[:, h * HEAD : (h + 1) * HEAD] = turned[
            h * tokens : (h + 1) * tokens
        ].astype(BF16)


VMEM = pl.BlockSpec(memory_space=pltpu.VMEM)
SMEM = pl.BlockSpec(memory_space=pltpu.SMEM)
PARAMS = pltpu.CompilerParams(vmem_limit_bytes=48 * 1024 * 1024)


def shape(dims, dtype):
    return jax.ShapeDtypeStruct(dims, dtype)


def on_device(
    x_in, dt_in, b_in, c_in, dy_in, a_log, d_skip, dt_bias,
    q_in, k_in, value_input, dout_in, doc_lengths, plan,
):
    seq_count = lax.axis_size("seq")
    own = lax.axis_index("seq").astype(jnp.int32).reshape(1)
    tokens, width = x_in.shape[1:]
    row_tokens = tokens * seq_count
    lengths = doc_lengths[0]
    x, dt, dy, b, c = x_in[0], dt_in[0], dy_in[0], b_in[0], c_in[0]
    bias, skip = dt_bias[None], d_skip[None]

    mixed = jnp.concatenate([q_in[0], k_in[0], value_input[0]], axis=1)
    gathered = lax.all_gather(mixed, "seq", axis=0, tiled=True)

    wide = functools.partial(pltpu.VMEM, dtype=F32)
    seg_shape = shape((NS, SEGS, width), F32)
    summary, seg_state, seg_adjoint, seg_delta = pl.pallas_call(
        summary_kernel,
        out_shape=(
            shape((SUMMARY_ROWS, width), BF16), seg_shape, seg_shape, shape((SEGS, width), F32),
        ),
        in_specs=[SMEM] * 2 + [VMEM] * 7,
        out_specs=[VMEM] * 4,
        scratch_shapes=[
            wide((NS, SEGS, width)),
            wide((NS, tokens, LANES)), wide((NS, tokens, LANES)),
            wide((tokens, width)), wide((tokens, width)), wide((tokens, width)),
            wide((SEGS, width)), wide((SEGS, width)),
        ],
        compiler_params=PARAMS,
        name="mixer_summary",
    )(own, lengths, x, dt, dy, b, c, a_log, bias)
    summaries = lax.all_gather(summary, "seq", axis=0)

    output, x_grad, dt_grad, bc_part, params_part = pl.pallas_call(
        mixer_kernel,
        out_shape=(
            shape((tokens, width), BF16), shape((tokens, width), BF16),
            shape((tokens, width), BF16), shape((2 * NS, tokens), F32),
            shape((NS + 2, width), F32),
        ),
        in_specs=[SMEM] * 2 + [VMEM] * 12,
        out_specs=[VMEM] * 5,
        scratch_shapes=[
            wide((NS, SEGS, width)), wide((NS, SEGS, width)),
            wide((NS, tokens, LANES)), wide((NS, tokens, LANES)),
            wide((tokens, width)), wide((tokens, width)),
            wide((tokens, width)), wide((tokens, width)),
            wide((NS, SEGS, width)), wide((NS, SEGS, width)),
            wide((tokens, width)), wide((tokens, width)), wide((tokens, width)),
            wide((NS, tokens, LANES)), wide((NS, tokens, LANES)),
            wide((NS, SEGS, width)),
        ],
        compiler_params=PARAMS,
        name="mixer",
    )(
        own, lengths, x, dt, dy, b, c, a_log, bias, skip,
        summaries, seg_state, seg_adjoint, seg_delta,
    )
    bc_sum = lax.psum(bc_part, "tp")
    params_row = lax.psum(params_part, "dp")
    params_sum = jnp.sum(lax.all_gather(params_row, "seq", axis=0), axis=0)

    attn_out, query_gradient, kv_part = pl.pallas_call(
        attention_kernel,
        out_shape=(
            shape((tokens, width), BF16), shape((tokens, width), BF16),
            shape((row_tokens, 2 * HEAD), BF16),
        ),
        in_specs=[SMEM] * 3 + [VMEM] * 2,
        out_specs=[VMEM] * 3,
        scratch_shapes=[
            pltpu.VMEM((HEAD, width // HEAD * tokens), BF16),
            pltpu.VMEM((HEAD, width // HEAD * tokens), BF16),
            wide((row_tokens, width // HEAD * tokens)),
            wide((width // HEAD * tokens, HEAD)),
            wide((HEAD, width // HEAD * tokens)),
            wide((HEAD, width // HEAD * tokens)),
        ],
        compiler_params=PARAMS,
        name="attention",
    )(own, lengths, plan[0], gathered, dout_in[0])
    kv_parts = lax.all_to_all(
        kv_part.reshape(seq_count, tokens, 2 * HEAD), "seq", split_axis=0, concat_axis=0
    )
    kv_sum = jnp.sum(kv_parts.astype(F32), axis=0).astype(BF16)
    return (
        output[None],
        x_grad[None],
        dt_grad[None],
        bc_sum[None, :NS],
        bc_sum[None, NS:],
        params_sum[:NS],
        params_sum[NS],
        params_sum[NS + 1],
        attn_out[None],
        query_gradient[None],
        kv_sum[None, :, :HEAD],
        kv_sum[None, :, HEAD:],
    )


def solution(mesh):
    tokens = P("dp", "seq", "tp")
    columns = P("dp", None, "seq")
    row = P("dp", None)
    return jax.shard_map(
        on_device,
        mesh=mesh,
        in_specs=(
            tokens, tokens, columns, columns, tokens, P(None, "tp"), P("tp"), P("tp"),
            tokens, tokens, tokens, tokens, row, row,
        ),
        out_specs=(
            tokens, tokens, tokens, columns, columns, P(None, "tp"), P("tp"), P("tp"),
            tokens, tokens, tokens, tokens,
        ),
        check_vma=False,
    )
```

time: 931 us -> 272 us (0.29)
  the two profiles are of different devices: /device:TPU:4 before, /device:TPU:32 now
where the time goes in v1:
time: 272 us
  blocking collectives  134 us (49%)
  waiting for transfers between devices  81.6 us (30%)
  Pallas kernels  23.9 us (9%)
  between operations  14.2 us (5%)
  starting transfers between devices  9.21 us (3%)
  local copies, waits for them, and re-layouts  6.58 us (2%)
    all_gather x1, waiting for transfers between devices, on_device(): gathered = lax.all_gather(mixed, 'seq', axis=0, tiled=True)  81.6 us
    all_gather x1, blocking collectives, on_device(): summaries = lax.all_gather(summary, 'seq', axis=0)  61 us
    all_gather x1, blocking collectives, on_device(): params_sum = jnp.sum(lax.all_gather(params_row, 'seq', axis=0), axis=0)  32.5 us
    psum x1, blocking collectives, on_device(): bc_sum = lax.psum(bc_part, 'tp')  23.5 us
    psum x1, blocking collectives, on_device(): params_row = lax.psum(params_part, 'dp')  17.3 us
    pallas_call x1, Pallas kernels, on_device(): pl.pallas_call(mixer_kernel, out_shape=(shape((tokens, width), BF16), sha...  11.1 us
    all_to_all x1, starting transfers between devices, on_device(): lax.all_to_all(kv_part.reshape(seq_count, tokens, 2 * HEAD), 'seq', split...  9.18 us
    pallas_call x1, Pallas kernels, on_device(): pl.pallas_call(attention_kernel, out_shape=(shape((tokens, width), BF16),...  9.17 us
  transfers between devices with their start and end apart: 2, of which 1 were waited for; matrix products, arithmetic and copies ran while one was open for 1% of the time, Pallas kernels for 5%

profile of v1, /device:TPU:32, one launch (start us, length us, event | category | flops | bytes accessed | tf_op | source)
XLA Modules:
  0.0 271.9 jit_solution(11438829906335750111)
XLA Ops:
  7.2 0.0 copy-start.10
  7.2 0.0 copy-start.5
  7.2 0.0 copy-start.8
  7.2 0.0 copy-start.3
  7.2 0.0 copy-start.7
  7.2 0.0 copy-start.6
  7.2 0.0 copy-start.2
  7.3 0.0 copy-start.1
  7.3 0.0 all-gather.3.cloned.1.call-start
  7.3 1.8 pad_maximum_fusion
  9.1 0.0 all-gather.3.cloned.1.call-update
  9.1 81.6 %all-gather.3.cloned.1.call-done.all_ref = bf16[2048,768]{1,0:T(8,128)(2,1)} async-done(((bf16[128,768]{1,0:T(8,128)(2,1)}), bf16[2048,768]{1,0:T(8,128)(2,1)}) %all-gather.3.cloned.1.call-update) | async-done | bytes 3145744 | tf_op jit(solution)/shard_map/all_gather | solution.py:401
  90.7 0.0 copy-start
  90.7 1.9 copy-done
  92.6 0.0 copy-start.4
  92.6 0.9 copy-done.4
  93.5 0.0 copy-start.9
  93.5 0.7 copy-done.9
  94.2 0.0 copy-start.12
  94.2 0.7 copy-done.12
  94.8 0.0 copy-start.11
  94.8 9.2 %attention.1 = (bf16[128,512]{1,0:T(8,128)(2,1)}, bf16[128,512]{1,0:T(8,128)(2,1)}, bf16[2048,256]{1,0:T(8,128)(2,1)}) custom-call(s32[1]{0:T(128)} %bitcast.own_ref, s32[8]{0:T(128)S(1)} %bitcast.47, s32[64]{0:T(128)S(1)} %bitcast.51, bf16[2048,768]{1,0:T(8,128)(2,1)S(1)} %copy-done, bf16[128,512]{1,0:T(8,128)(2,1)S(1)} %bitcast.39), custom_call_target="tpu_custom_call" | custom-call | tf_op jit(solution)/shard_map/attention/pallas_call | solution.py:452
  104.0 9.2 %all-to-all-start = ((bf16[16,128,256]{2,1,0:T(8,128)(2,1)}), bf16[16,128,256]{2,1,0:T(8,128)(2,1)S(1)}, u32[]{:S(2)}, u32[]{:S(2)}) async-start(bf16[16,128,256]{2,1,0:T(8,128)(2,1)} %bitcast.25), calls=%async_computation | async-start | bytes 2097152 | tf_op jit(solution)/shard_map/all_to_all | solution.py:471
  113.2 0.0 copy-done.10
  113.2 0.0 copy-done.5
  113.2 0.0 copy-done.8
  113.2 0.0 copy-done.3
  113.2 0.0 copy-done.7
  113.2 0.0 copy-done.6
  113.2 0.0 copy-done.2
  113.3 0.0 copy-done.1
  113.3 3.7 %mixer_summary.1 = (bf16[48,512]{1,0:T(8,128)(2,1)S(1)}, f32[16,8,512]{2,1,0:T(8,128)S(1)}, f32[16,8,512]{2,1,0:T(8,128)S(1)}, f32[8,512]{1,0:T(8,128)S(1)}) custom-call(s32[1]{0:T(128)} %bitcast.own_ref, s32[8]{0:T(128)S(1)} %bitcast.48, bf16[128,512]{1,0:T(8,128)(2,1)S(1)} %bitcast.33, bf16[128,512]{1,0:T(8,128)(2,1)S(1)} %bitcast.35, ...), custom_call_target="tpu_custom_call" | custom-call | tf_op jit(solution)/shard_map/mixer_summary/pallas_call | solution.py:405
  116.9 61.0 %all-gather = bf16[768,512]{1,0:T(8,128)(2,1)S(1)} all-gather(bf16[48,512]{1,0:T(8,128)(2,1)S(1)} %get-tuple-element.24), channel_id=2, replica_groups=mesh['seq'=16,'tp'=8,'dp'=4] {'seq'}, dimensions={0}, use_global_device_ids=true | all-gather | bytes 835584 | tf_op jit(solution)/shard_map/all_gather | solution.py:421
  177.9 0.0 copy-done.11
  177.9 11.1 %mixer.1 = (bf16[128,512]{1,0:T(8,128)(2,1)}, bf16[128,512]{1,0:T(8,128)(2,1)}, bf16[128,512]{1,0:T(8,128)(2,1)}, f32[32,128]{1,0:T(8,128)S(1)}, f32[18,512]{1,0:T(8,128)S(1)}) custom-call(s32[1]{0:T(128)} %bitcast.own_ref, s32[8]{0:T(128)S(1)} %bitcast.49, bf16[128,512]{1,0:T(8,128)(2,1)S(1)} %bitcast.34, bf16[128,512]{1,0:T(8,128)(2,1)S(1)} %bitcast.36, ...), custom_call_target="tpu_custom_call" | custom-call | tf_op jit(solution)/shard_map/mixer/pallas_call | solution.py:423
  188.9 17.3 %psum.15 = f32[1,18,512]{2,1,0:T(8,128)S(1)} all-reduce(f32[1,18,512]{2,1,0:T(8,128)S(1)} %bitcast.40), channel_id=1, replica_groups=mesh['seq'=16,'tp'=8,'dp'=4] {'dp'}, use_global_device_ids=true, to_apply=%region_1.0 | all-reduce | flops 9216 | bytes 73728 | tf_op jit(solution)/shard_map/psum | solution.py:449
  206.3 32.5 %all_gather.18 = f32[16,18,512]{2,1,0:T(8,128)S(1)} all-gather(f32[1,18,512]{2,1,0:T(8,128)S(1)} %psum.15), channel_id=1, replica_groups=mesh['seq'=16,'tp'=8,'dp'=4] {'seq'}, dimensions={0}, use_global_device_ids=true | all-gather | bytes 626688 | tf_op jit(solution)/shard_map/all_gather | solution.py:450
  238.8 0.1 reduce_sum.21
  238.9 0.6 slice.30
  239.5 23.5 %psum.14 = f32[32,128]{1,0:T(8,128)S(1)} all-reduce(f32[32,128]{1,0:T(8,128)S(1)} %get-tuple-element.31), channel_id=1, replica_groups=mesh['seq'=16,'tp'=8,'dp'=4] {'tp'}, use_global_device_ids=true, to_apply=%region_0.0 | all-reduce | flops 4096 | bytes 32768 | tf_op jit(solution)/shard_map/psum | solution.py:448
  263.0 0.6 fusion
  263.6 0.6 slice_bitcast_fusion.2
  264.2 0.0 all-to-all-done
  264.2 0.1 reduce_sum.22
  264.4 0.6 slice_bitcast_fusion
Async XLA Ops:
  7.2 106.0 %copy-start.10 = (s32[1,8]{1,0:T(1,128)S(1)}, s32[1,8]{1,0:T(1,128)}, u32[]{:S(2)}) copy-start(s32[1,8]{1,0:T(1,128)} %param.26) | copy-start | bytes 100
  7.2 106.0 %copy-start.5 = (f32[16,512]{1,0:T(8,128)S(1)}, f32[16,512]{1,0:T(8,128)}, u32[]{:S(2)}) copy-start(f32[16,512]{1,0:T(8,128)} %a_ref.3) | copy-start | bytes 98308
  7.2 106.0 %copy-start.8 = (f32[512]{0:T(512)S(1)}, f32[512]{0:T(512)}, u32[]{:S(2)}) copy-start(f32[512]{0:T(512)} %param.21) | copy-start | bytes 6148
  7.2 106.0 %copy-start.3 = (bf16[1,128,512]{2,1,0:T(8,128)(2,1)S(1)}, bf16[1,128,512]{2,1,0:T(8,128)(2,1)}, u32[]{:S(2)}) copy-start(bf16[1,128,512]{2,1,0:T(8,128)(2,1)} %param.18) | copy-start | bytes 393220
  7.2 106.0 %copy-start.7 = (bf16[1,16,128]{2,1,0:T(8,128)(2,1)S(1)}, bf16[1,16,128]{2,1,0:T(8,128)(2,1)}, u32[]{:S(2)}) copy-start(bf16[1,16,128]{2,1,0:T(8,128)(2,1)} %param.17) | copy-start | bytes 12292
  7.2 106.0 %copy-start.6 = (bf16[1,16,128]{2,1,0:T(8,128)(2,1)S(1)}, bf16[1,16,128]{2,1,0:T(8,128)(2,1)}, u32[]{:S(2)}) copy-start(bf16[1,16,128]{2,1,0:T(8,128)(2,1)} %param.16) | copy-start | bytes 12292
  7.2 106.0 %copy-start.2 = (bf16[1,128,512]{2,1,0:T(8,128)(2,1)S(1)}, bf16[1,128,512]{2,1,0:T(8,128)(2,1)}, u32[]{:S(2)}) copy-start(bf16[1,128,512]{2,1,0:T(8,128)(2,1)} %param.15) | copy-start | bytes 393220
  7.3 106.0 %copy-start.1 = (bf16[1,128,512]{2,1,0:T(8,128)(2,1)S(1)}, bf16[1,128,512]{2,1,0:T(8,128)(2,1)}, u32[]{:S(2)}) copy-start(bf16[1,128,512]{2,1,0:T(8,128)(2,1)} %param.14) | copy-start | bytes 393220
  7.3 83.5 %all-gather.3.cloned.1.call-start = ((), (), s32[]{:S(2)}) async-start(), calls=%async_computation.1 | async-start | bytes 3342336 | tf_op jit(solution)/shard_map/all_gather | solution.py:401
  90.7 1.9 copy-start
  92.6 0.9 copy-start.4
  93.5 0.7 copy-start.9
  94.2 0.7 copy-start.12
  94.8 83.1 %copy-start.11 = (f32[512]{0:T(512)S(1)}, f32[512]{0:T(512)}, u32[]{:S(2)}) copy-start(f32[512]{0:T(512)} %param.20) | copy-start | bytes 6148
  104.0 160.2 %all-to-all-start = ((bf16[16,128,256]{2,1,0:T(8,128)(2,1)}), bf16[16,128,256]{2,1,0:T(8,128)(2,1)S(1)}, u32[]{:S(2)}, u32[]{:S(2)}) async-start(bf16[16,128,256]{2,1,0:T(8,128)(2,1)} %bitcast.25), calls=%async_computation | async-start | bytes 2097152 | tf_op jit(solution)/shard_map/all_to_all | solution.py:471
Sparse Core Ops, SparseCore 0:
  10.2 80.5 all-gather.2

commit v2 on v1

--- a/solution.py
+++ b/solution.py
@@ -445,9 +445,8 @@
         own, lengths, x, dt, dy, b, c, a_log, bias, skip,
         summaries, seg_state, seg_adjoint, seg_delta,
     )
-    bc_sum = lax.psum(bc_part, "tp")
-    params_row = lax.psum(params_part, "dp")
-    params_sum = jnp.sum(lax.all_gather(params_row, "seq", axis=0), axis=0)
+    params_row = jnp.sum(lax.all_gather(params_part, "seq", axis=0), axis=0)
+    gathered, params_row = lax.optimization_barrier((gathered, params_row))
 
     attn_out, query_gradient, kv_part = pl.pallas_call(
         attention_kernel,
@@ -468,9 +467,12 @@
         compiler_params=PARAMS,
         name="attention",
     )(own, lengths, plan[0], gathered, dout_in[0])
+    kv_part, bc_part, params_row = lax.optimization_barrier((kv_part, bc_part, params_row))
     kv_parts = lax.all_to_all(
         kv_part.reshape(seq_count, tokens, 2 * HEAD), "seq", split_axis=0, concat_axis=0
     )
+    bc_sum = lax.psum(bc_part, "tp")
+    params_sum = lax.psum(params_row, "dp")
     kv_sum = jnp.sum(kv_parts.astype(F32), axis=0).astype(BF16)
     return (
         output[None],

time: 272 us -> 180 us (0.66)
  waiting for transfers between devices: 81.6 us -> 0.04 us
  blocking collectives: 134 us -> 119 us
  local copies, waits for them, and re-layouts: 6.58 us -> 11.2 us
    all_gather x1, waiting for transfers between devices: 81.6 us -> 0.02 us  [on_device(): gathered = lax.all_gather(mixed, 'seq', axis=0, tiled=True)]
    all_gather x1, blocking collectives: 61 us -> 43.8 us  [on_device(): summaries = lax.all_gather(summary, 'seq', axis=0)]
    unnamed x26, local copies, waits for them, and re-layouts: 4.14 us -> 8.75 us
  transfers between devices with their start and end apart: 2 -> 2, of which waited for: 1 -> 0; matrix products, arithmetic and copies ran while one was open for 1% -> 1% of each run, Pallas kernels for 5% -> 8%
where the time goes in v2:
time: 180 us; the launch traced here: 179 us
  blocking collectives  119 us (66%)
  Pallas kernels  24.9 us (14%)
  between operations  14.1 us (8%)
  local copies, waits for them, and re-layouts  11.2 us (6%)
  starting transfers between devices  7.78 us (4%)
  other arithmetic  1.89 us (1%)
    all_gather x1, blocking collectives, on_device(): summaries = lax.all_gather(summary, 'seq', axis=0)  43.8 us
    all_gather x1, blocking collectives, on_device(): params_row = jnp.sum(lax.all_gather(params_part, 'seq', axis=0), axis=0)  33.6 us
    psum x1, blocking collectives, on_device(): bc_sum = lax.psum(bc_part, 'tp')  24.7 us
    psum x1, blocking collectives, on_device(): params_sum = lax.psum(params_row, 'dp')  17.1 us
    pallas_call x1, Pallas kernels, on_device(): pl.pallas_call(mixer_kernel, out_shape=(shape((tokens, width), BF16), sha...  11 us
    pallas_call x1, Pallas kernels, on_device(): pl.pallas_call(attention_kernel, out_shape=(shape((tokens, width), BF16),...  10.2 us
    unnamed x26, local copies, waits for them, and re-layouts  8.75 us
    all_to_all x1, starting transfers between devices, on_device(): lax.all_to_all(kv_part.reshape(seq_count, tokens, 2 * HEAD), 'seq', split...  7.74 us
  transfers between devices with their start and end apart: 2, of which 0 were waited for; matrix products, arithmetic and copies ran while one was open for 1% of the time, Pallas kernels for 8%

profile of v2, /device:TPU:32, one launch (start us, length us, event | category | flops | bytes accessed | tf_op | source)
XLA Modules:
  0.0 179.1 jit_solution(9317220875976345474)
XLA Ops:
  7.2 0.0 copy-start.10
  7.2 0.0 copy-start.12
  7.2 0.0 copy-start.4
  7.2 0.0 all-gather.5.cloned.1.call-start
  7.3 1.7 pad_maximum_fusion
  8.9 0.0 all-gather.5.cloned.1.call-update
  9.0 0.0 copy-start.1
  9.0 0.9 copy-done.1
  9.9 0.0 copy-start.2
  9.9 0.9 copy-done.2
  10.8 0.0 copy-start.3
  10.8 0.9 copy-done.3
  11.7 0.0 copy-start.5
  11.7 0.8 copy-done.5
  12.4 0.0 copy-start.6
  12.4 0.7 copy-done.6
  13.1 0.0 copy-start.7
  13.1 0.7 copy-done.7
  13.8 0.0 copy-start.8
  13.8 0.7 copy-done.8
  14.5 0.0 copy-start.9
  14.5 0.7 copy-done.9
  15.2 3.7 %mixer_summary.1 = (bf16[48,512]{1,0:T(8,128)(2,1)S(1)}, f32[16,8,512]{2,1,0:T(8,128)S(1)}, f32[16,8,512]{2,1,0:T(8,128)S(1)}, f32[8,512]{1,0:T(8,128)S(1)}) custom-call(s32[1]{0:T(128)} %bitcast.own_ref, s32[8]{0:T(128)S(1)} %bitcast.47, bf16[128,512]{1,0:T(8,128)(2,1)S(1)} %bitcast.33, bf16[128,512]{1,0:T(8,128)(2,1)S(1)} %bitcast.35, ...), custom_call_target="tpu_custom_call" | custom-call | tf_op jit(solution)/shard_map/mixer_summary/pallas_call | solution.py:405
  18.8 43.8 %all-gather = bf16[768,512]{1,0:T(8,128)(2,1)S(1)} all-gather(bf16[48,512]{1,0:T(8,128)(2,1)S(1)} %get-tuple-element.29), channel_id=2, replica_groups=mesh['seq'=16,'tp'=8,'dp'=4] {'seq'}, dimensions={0}, use_global_device_ids=true | all-gather | bytes 835584 | tf_op jit(solution)/shard_map/all_gather | solution.py:421
  62.6 0.0 copy-start.11
  62.6 0.7 copy-done.11
  63.3 11.0 %mixer.1 = (bf16[128,512]{1,0:T(8,128)(2,1)}, bf16[128,512]{1,0:T(8,128)(2,1)}, bf16[128,512]{1,0:T(8,128)(2,1)}, f32[32,128]{1,0:T(8,128)S(1)}, f32[18,512]{1,0:T(8,128)S(1)}) custom-call(s32[1]{0:T(128)} %bitcast.own_ref, s32[8]{0:T(128)S(1)} %bitcast.48, bf16[128,512]{1,0:T(8,128)(2,1)S(1)} %bitcast.34, bf16[128,512]{1,0:T(8,128)(2,1)S(1)} %bitcast.36, ...), custom_call_target="tpu_custom_call" | custom-call | tf_op jit(solution)/shard_map/mixer/pallas_call | solution.py:423
  74.3 33.6 %all-gather.2 = f32[16,18,512]{2,1,0:T(8,128)S(1)} all-gather(f32[1,18,512]{2,1,0:T(8,128)S(1)} %bitcast.40), channel_id=3, replica_groups=mesh['seq'=16,'tp'=8,'dp'=4] {'seq'}, dimensions={0}, use_global_device_ids=true | all-gather | bytes 626688 | tf_op jit(solution)/shard_map/all_gather | solution.py:448
  107.9 0.1 reduce_sum.21
  108.0 0.0 all-gather.5.cloned.1.call-done.all_ref
  108.0 0.0 copy-done.10
  108.0 0.0 copy-done.12
  108.0 0.0 copy-done.4
  108.1 0.0 copy-start
  108.1 1.9 %copy-done = bf16[2048,768]{1,0:T(8,128)(2,1)S(1)} copy-done((bf16[2048,768]{1,0:T(8,128)(2,1)S(1)}, bf16[2048,768]{1,0:T(8,128)(2,1)}, u32[]{:S(2)}) %copy-start) | copy-done | bytes 3145752
  109.9 10.2 %attention.1 = (bf16[128,512]{1,0:T(8,128)(2,1)}, bf16[128,512]{1,0:T(8,128)(2,1)}, bf16[2048,256]{1,0:T(8,128)(2,1)}) custom-call(s32[1]{0:T(128)} %bitcast.own_ref, s32[8]{0:T(128)S(1)} %bitcast.49, s32[64]{0:T(128)S(1)} %bitcast.51, bf16[2048,768]{1,0:T(8,128)(2,1)S(1)} %copy-done, bf16[128,512]{1,0:T(8,128)(2,1)S(1)} %bitcast.39), custom_call_target="tpu_custom_call" | custom-call | tf_op jit(solution)/shard_map/attention/pallas_call | solution.py:451
  120.1 7.7 %all-to-all-start = ((bf16[16,128,256]{2,1,0:T(8,128)(2,1)}), bf16[16,128,256]{2,1,0:T(8,128)(2,1)S(1)}, u32[]{:S(2)}, u32[]{:S(2)}) async-start(bf16[16,128,256]{2,1,0:T(8,128)(2,1)} %bitcast.25), calls=%async_computation | async-start | bytes 2097152 | tf_op jit(solution)/shard_map/all_to_all | solution.py:471
  127.9 17.1 %psum.15 = f32[18,512]{1,0:T(8,128)S(1)} all-reduce(f32[18,512]{1,0:T(8,128)S(1)} %reduce_sum.21), channel_id=1, replica_groups=mesh['seq'=16,'tp'=8,'dp'=4] {'dp'}, use_global_device_ids=true, to_apply=%region_2.0 | all-reduce | flops 9216 | bytes 73728 | tf_op jit(solution)/shard_map/psum | solution.py:475
  144.9 0.6 slice.30
  145.6 24.7 %psum.14 = f32[32,128]{1,0:T(8,128)S(1)} all-reduce(f32[32,128]{1,0:T(8,128)S(1)} %get-tuple-element.41), channel_id=1, replica_groups=mesh['seq'=16,'tp'=8,'dp'=4] {'tp'}, use_global_device_ids=true, to_apply=%region_1.0 | all-reduce | flops 4096 | bytes 32768 | tf_op jit(solution)/shard_map/psum | solution.py:474
  170.3 0.6 fusion
  170.9 0.6 slice_bitcast_fusion.2
  171.5 0.0 all-to-all-done
  171.5 0.1 reduce_sum.22
  171.6 0.6 slice_bitcast_fusion
Async XLA Ops:
  7.2 100.8 %copy-start.10 = (s32[1,8]{1,0:T(1,128)S(1)}, s32[1,8]{1,0:T(1,128)}, u32[]{:S(2)}) copy-start(s32[1,8]{1,0:T(1,128)} %param.26) | copy-start | bytes 100
  7.2 100.8 %copy-start.12 = (s32[1,64]{1,0:T(1,128)S(1)}, s32[1,64]{1,0:T(1,128)}, u32[]{:S(2)}) copy-start(s32[1,64]{1,0:T(1,128)} %param.27) | copy-start | bytes 772
  7.2 100.8 %copy-start.4 = (bf16[1,128,512]{2,1,0:T(8,128)(2,1)S(1)}, bf16[1,128,512]{2,1,0:T(8,128)(2,1)}, u32[]{:S(2)}) copy-start(bf16[1,128,512]{2,1,0:T(8,128)(2,1)} %param.25) | copy-start | bytes 393220
  7.2 100.8 %all-gather.5.cloned.1.call-start = ((), (), s32[]{:S(2)}) async-start(), calls=%async_computation.1 | async-start | bytes 3342336 | tf_op jit(solution)/shard_map/all_gather | solution.py:401
  9.0 0.9 copy-start.1
  9.9 0.9 copy-start.2
  10.8 0.9 copy-start.3
  11.7 0.8 copy-start.5
  12.4 0.7 copy-start.6
  13.1 0.7 copy-start.7
  13.8 0.7 copy-start.8
  14.5 0.7 copy-start.9
  62.6 0.7 copy-start.11
  108.1 1.9 %copy-start = (bf16[2048,768]{1,0:T(8,128)(2,1)S(1)}, bf16[2048,768]{1,0:T(8,128)(2,1)}, u32[]{:S(2)}) copy-start(bf16[2048,768]{1,0:T(8,128)(2,1)} %all-gather.5.cloned.1.call-done.all_ref) | copy-start | bytes 9437188
  120.1 51.3 %all-to-all-start = ((bf16[16,128,256]{2,1,0:T(8,128)(2,1)}), bf16[16,128,256]{2,1,0:T(8,128)(2,1)S(1)}, u32[]{:S(2)}, u32[]{:S(2)}) async-start(bf16[16,128,256]{2,1,0:T(8,128)(2,1)} %bitcast.25), calls=%async_computation | async-start | bytes 2097152 | tf_op jit(solution)/shard_map/all_to_all | solution.py:471
Sparse Core Ops, SparseCore 0:
  10.1 83.8 all-gather.4

commit v3 on v1

v3 whole, which is shorter than its diff:
```python
import jax
import jax.numpy as jnp
from jax import lax
from jax.experimental import pallas as pl
from jax.experimental.pallas import tpu as pltpu
from jax.sharding import PartitionSpec as P

NS = 16
HEAD = 128
BLOCK = 32
LANES = 128
SEGS = 8
RESET = 1e30
LOG2E = 1.4426950408889634
NEG = -1e30
SUMMARY_ROWS = 48

F32 = jnp.float32
BF16 = jnp.bfloat16


def dot(a, b, dims=((1,), (0,)), precision=None):
    return lax.dot_general(a, b, (dims, ((), ())), precision=precision, preferred_element_type=F32)


def exact_dot(a, b, dims=((1,), (0,))):
    return dot(a, b, dims, lax.Precision.HIGHEST)


def iota(shape, axis):
    return lax.broadcasted_iota(jnp.int32, shape, axis)


def to_segments(tokens):
    span = tokens // SEGS
    row = iota((tokens, tokens), 0)
    token = iota((tokens, tokens), 1)
    return jnp.where(token == lax.rem(row, SEGS) * span + lax.div(row, SEGS), 1.0, 0.0)


def to_tokens(tokens):
    span = tokens // SEGS
    token = iota((tokens, tokens), 0)
    row = iota((tokens, tokens), 1)
    return jnp.where(row == lax.rem(token, span) * SEGS + lax.div(token, span), 1.0, 0.0)


def starts_of(lengths_ref):
    starts = [jnp.int32(0)]
    for k in range(lengths_ref.shape[1] - 1):
        starts.append(starts[-1] + lengths_ref[0, k])
    return starts


def begin_copies(pairs, semaphores):
    copies = [
        pltpu.make_async_copy(source, target, semaphores.at[k])
        for k, (source, target) in enumerate(pairs)
    ]
    for copy in copies:
        copy.start()
    return copies


def wait_all(copies):
    for copy in copies:
        copy.wait()


def softplus_of(raw):
    small = jnp.exp(-jnp.abs(raw))
    one = 1.0 + small
    tail = one - 1.0
    safe = jnp.where(tail == 0.0, 1.0, tail)
    log1p = jnp.where(tail == 0.0, small, jnp.log(one) * (small / safe))
    return jnp.maximum(raw, 0.0) + log1p


def with_resets(own_ref, lengths_ref, delta):
    tokens = delta.shape[0]
    span = tokens // SEGS
    row = iota(delta.shape, 0)
    token = own_ref[0] * tokens + lax.rem(row, SEGS) * span + lax.div(row, SEGS)
    first = token == 0
    for start in starts_of(lengths_ref):
        first = first | (token == start)
    return jnp.where(first, RESET, delta)


def spread(source, target):
    for n in range(NS):
        target[n] = jnp.broadcast_to(source[n : n + 1], target.shape[1:])


def fill_columns(segment, b_ref, c_ref, b_wide, c_wide):
    tokens = segment.shape[0]
    for source, target in ((b_ref, b_wide), (c_ref, c_wide)):
        columns = dot(segment, source[...], ((1,), (1,)))
        for n in range(NS):
            target[n] = jnp.broadcast_to(columns[:, n : n + 1], (tokens, LANES))


def shifted(value, by, fill):
    rows = value.shape[0]
    row = iota(value.shape, 0)
    moved = pltpu.roll(value, by % rows, 0)
    return jnp.where((row >= by) & (row < rows + by), moved, fill)


def summary_kernel(
    own_ref, lengths_hbm, x_hbm, dt_hbm, dy_hbm, b_hbm, c_hbm, a_hbm, bias_hbm,
    summary_ref, seg_state_ref, seg_adjoint_ref, seg_delta_ref,
    lengths_ref, x_ref, dt_ref, dy_ref, b_ref, c_ref, a_ref, bias_ref,
    rate2_ref, b_wide, c_wide, decay_delta, drive, upstream, before_ref, after_ref, rows_ref, semaphores,
):
    tokens, width = x_ref.shape
    span = tokens // SEGS
    copies = begin_copies(
        (
            (dt_hbm.at[0], dt_ref), (bias_hbm, bias_ref), (lengths_hbm, lengths_ref),
            (x_hbm.at[0], x_ref), (dy_hbm.at[0], dy_ref), (a_hbm, a_ref),
            (b_hbm.at[0], b_ref), (c_hbm.at[0], c_ref),
        ),
        semaphores,
    )
    segment = to_segments(tokens).astype(BF16)
    wait_all(copies[:3])
    raw = dot(segment, dt_ref[...]) + bias_ref[...]
    delta = softplus_of(raw)
    reset_delta = with_resets(own_ref, lengths_ref, delta)
    decay_delta[...] = reset_delta
    wait_all(copies[3:])
    drive[...] = delta * dot(segment, x_ref[...])
    upstream[...] = dot(segment, dy_ref[...])
    spread(-jnp.exp(a_ref[...]) * LOG2E, rate2_ref)
    fill_columns(segment, b_ref, c_ref, b_wide, c_wide)

    total = reset_delta[:SEGS]
    for pos in range(1, span):
        total = total + reset_delta[pos * SEGS : (pos + 1) * SEGS]
    seg_delta_ref[...] = total
    after = shifted(total, -1, 0.0)
    before = shifted(total, 1, 0.0)
    for by in (1, 2, 4):
        after = after + shifted(after, -by, 0.0)
        before = before + shifted(before, by, 0.0)
    after_ref[...] = after
    before_ref[...] = before
    whole = before[SEGS - 1 :] + total[SEGS - 1 :]
    high = whole.astype(BF16)
    low = (whole - high.astype(F32)).astype(BF16)
    summary_ref[2 * NS :] = jnp.zeros((SUMMARY_ROWS - 2 * NS, width), BF16)
    summary_ref[2 * NS : 2 * NS + 1] = high
    summary_ref[2 * NS + 1 : 2 * NS + 2] = low

    def state_row(n, carry):
        state_rows, adjoint_rows = [], []
        for lane in range(0, width, 4 * LANES):
            groups = [slice(k, k + LANES) for k in range(lane, lane + 4 * LANES, LANES)]
            rate2 = [rate2_ref[n, :, cols] for cols in groups]
            state = [jnp.zeros((SEGS, LANES), F32) for _ in groups]
            adjoint = list(state)
            decays = []
            for pos in range(span):
                rows = slice(pos * SEGS, (pos + 1) * SEGS)
                b_col = b_wide[n, rows]
                decays.append([])
                for k, cols in enumerate(groups):
                    decay = jnp.exp2(rate2[k] * decay_delta[rows, cols])
                    decays[pos].append(decay)
                    state[k] = decay * state[k] + b_col * drive[rows, cols]
            for pos in reversed(range(span)):
                rows = slice(pos * SEGS, (pos + 1) * SEGS)
                c_col = c_wide[n, rows]
                for k, cols in enumerate(groups):
                    adjoint[k] = decays[pos][k] * (c_col * upstream[rows, cols] + adjoint[k])
            for k, cols in enumerate(groups):
                seg_state_ref[n, :, cols] = state[k]
                seg_adjoint_ref[n, :, cols] = adjoint[k]
                weight = jnp.exp2(rate2[k] * after_ref[:, cols])
                state_rows.append(jnp.sum(weight * state[k], axis=0, keepdims=True))
                weight = jnp.exp2(rate2[k] * before_ref[:, cols])
                adjoint_rows.append(jnp.sum(weight * adjoint[k], axis=0, keepdims=True))
        rows_ref[n] = jnp.broadcast_to(jnp.concatenate(state_rows, 1), (SEGS, width))
        rows_ref[NS + n] = jnp.broadcast_to(jnp.concatenate(adjoint_rows, 1), (SEGS, width))
        return carry

    lax.fori_loop(0, NS, state_row, 0)
    gathered = jnp.concatenate([rows_ref[n, :1] for n in range(2 * NS)], 0)
    summary_ref[: 2 * NS] = gathered.astype(BF16)


def mixer_kernel(
    own_ref, lengths_hbm, x_hbm, dt_hbm, dy_hbm, b_hbm, c_hbm, a_hbm, bias_hbm, skip_hbm,
    summaries_hbm, seg_state_hbm, seg_adjoint_hbm, seg_delta_hbm,
    out_ref, x_grad_ref, dt_grad_ref, bc_ref, params_ref,
    lengths_ref, x_ref, dt_ref, dy_ref, b_ref, c_ref, a_ref, bias_ref, skip_ref,
    summaries_ref, seg_state_ref, seg_adjoint_ref, seg_delta_ref,
    rate_ref, enter_ref, arrive_ref, b_wide, c_wide,
    delta_ref, decay_delta, drive, upstream, y_acc, xg_acc, dd_acc, bg_acc, cg_acc, rate_acc,
    semaphores,
):
    tokens, width = x_ref.shape
    span = tokens // SEGS
    count = summaries_ref.shape[0]
    own = own_ref[0]
    copies = begin_copies(
        (
            (dt_hbm.at[0], dt_ref), (bias_hbm, bias_ref), (lengths_hbm, lengths_ref),
            (a_hbm, a_ref), (summaries_hbm, summaries_ref),
            (x_hbm.at[0], x_ref), (dy_hbm.at[0], dy_ref), (skip_hbm, skip_ref),
            (b_hbm.at[0], b_ref), (c_hbm.at[0], c_ref),
            (seg_state_hbm, seg_state_ref), (seg_adjoint_hbm, seg_adjoint_ref),
            (seg_delta_hbm, seg_delta_ref),
        ),
        semaphores,
    )
    segment = to_segments(tokens).astype(BF16)
    wait_all(copies[:3])
    delta = softplus_of(dot(segment, dt_ref[...]) + bias_ref[...])
    delta_ref[...] = delta
    decay_delta[...] = with_resets(own_ref, lengths_ref, delta)
    wait_all(copies[3:])
    drive[...] = delta * dot(segment, x_ref[...])
    upstream[...] = dot(segment, dy_ref[...])
    fill_columns(segment, b_ref, c_ref, b_wide, c_wide)
    rate_all = -jnp.exp(a_ref[...])
    rate2_all = rate_all * LOG2E
    spread(rate_all, rate_ref)

    entering = jnp.zeros((NS, width), F32)
    arriving = jnp.zeros((NS, width), F32)

    def factor(j):
        ends = summaries_ref[j, 2 * NS : 2 * NS + 2].astype(F32)
        return jnp.exp2(rate2_all * (ends[0:1] + ends[1:2]))

    for j in range(count - 1):
        longer = factor(j) * entering + summaries_ref[j, :NS].astype(F32)
        entering = jnp.where(j < own, longer, entering)
    for j in reversed(range(1, count)):
        longer = factor(j) * arriving + summaries_ref[j, NS : 2 * NS].astype(F32)
        arriving = jnp.where(j > own, longer, arriving)
    spread(entering, enter_ref)
    spread(arriving, arrive_ref)

    y_acc[...] = jnp.zeros_like(y_acc)
    xg_acc[...] = jnp.zeros_like(xg_acc)
    dd_acc[...] = jnp.zeros_like(dd_acc)

    def state_row(n, carry):
        row = iota((SEGS, LANES), 0)
        for lane in range(0, width, 4 * LANES):
            groups = [slice(k, k + LANES) for k in range(lane, lane + 4 * LANES, LANES)]
            rate = [rate_ref[n, :, cols] for cols in groups]
            rate2 = [value * LOG2E for value in rate]
            state, adjoint = [], []
            for k, cols in enumerate(groups):
                seg_factor = jnp.exp2(rate2[k] * seg_delta_ref[:, cols])
                edge = enter_ref[n, :, cols]
                scale, total = seg_factor, seg_state_ref[n, :, cols]
                for by in (1, 2, 4):
                    total = total + scale * shifted(total, by, 0.0)
                    scale = scale * shifted(scale, by, 1.0)
                moved = pltpu.roll(total + scale * edge, 1, 0)
                state.append(jnp.where(row == 0, edge, moved))
                edge = arrive_ref[n, :, cols]
                scale, total = seg_factor, seg_adjoint_ref[n, :, cols]
                for by in (1, 2, 4):
                    total = total + scale * shifted(total, -by, 0.0)
                    scale = scale * shifted(scale, -by, 1.0)
                moved = pltpu.roll(total + scale * edge, SEGS - 1, 0)
                adjoint.append(jnp.where(row == SEGS - 1, edge, moved))
            decays, befores = [], []
            for pos in range(span):
                rows = slice(pos * SEGS, (pos + 1) * SEGS)
                b_col, c_col = b_wide[n, rows], c_wide[n, rows]
                decays.append([])
                befores.append(list(state))
                part = None
                for k, cols in enumerate(groups):
                    decay = jnp.exp2(rate2[k] * decay_delta[rows, cols])
                    decays[pos].append(decay)
                    state[k] = decay * state[k] + b_col * drive[rows, cols]
                    y_acc[rows, cols] += c_col * state[k]
                    term = upstream[rows, cols] * state[k]
                    part = term if part is None else part + term
                if lane == 0:
                    cg_acc[n, rows] = part
                else:
                    cg_acc[n, rows] += part
            rate_sum = [jnp.zeros((SEGS, LANES), F32) for _ in groups]
            for pos in reversed(range(span)):
                rows = slice(pos * SEGS, (pos + 1) * SEGS)
                b_col, c_col = b_wide[n, rows], c_wide[n, rows]
                part = None
                for k, cols in enumerate(groups):
                    full = c_col * upstream[rows, cols] + adjoint[k]
                    adjoint[k] = decays[pos][k] * full
                    xg_acc[rows, cols] += full * b_col
                    term = full * drive[rows, cols]
                    part = term if part is None else part + term
                    through = adjoint[k] * befores[pos][k]
                    dd_acc[rows, cols] += rate[k] * through
                    rate_sum[k] = rate_sum[k] + delta_ref[rows, cols] * through
                if lane == 0:
                    bg_acc[n, rows] = part
                else:
                    bg_acc[n, rows] += part
            for k, cols in enumerate(groups):
                rate_acc[n, :, cols] = rate[k] * rate_sum[k]
        return carry

    lax.fori_loop(0, NS, state_row, 0)

    token = to_tokens(tokens).astype(BF16)
    inputs = dot(segment, x_ref[...])
    skip = skip_ref[...]
    out_ref[...] = dot(token, (y_acc[...] + skip * inputs).astype(BF16)).astype(BF16)
    x_grad = xg_acc[...] * delta_ref[...] + skip * upstream[...]
    x_grad_ref[...] = dot(token, x_grad.astype(BF16)).astype(BF16)
    raw = dot(segment, dt_ref[...]) + bias_ref[...]
    raw_grad = (xg_acc[...] * inputs + dd_acc[...]) / (1.0 + jnp.exp(-raw))
    dt_grad_ref[...] = dot(token, raw_grad.astype(BF16)).astype(BF16)
    params_ref[:NS] = jnp.sum(rate_acc[...], axis=1)
    params_ref[NS : NS + 1] = jnp.sum(upstream[...] * inputs, axis=0, keepdims=True)
    params_ref[NS + 1 : NS + 2] = jnp.sum(raw_grad, axis=0, keepdims=True)
    lane = iota((tokens, LANES), 1)
    sums = jnp.zeros((tokens, LANES), F32)
    for k, source in enumerate((bg_acc, cg_acc)):
        for n in range(NS):
            total = jnp.sum(source[n], axis=1, keepdims=True)
            sums = jnp.where(lane == k * NS + n, total, sums)
    bc_ref[...] = exact_dot(sums.T[: 2 * NS], to_segments(tokens))


def by_head(ref):
    value = ref[...]
    return jnp.concatenate(
        [value[:, h : h + HEAD] for h in range(0, value.shape[1], HEAD)], 0
    )


def turn_back(ref, turned):
    tokens, width = ref.shape
    for h in range(width // HEAD):
        ref[:, h * HEAD : (h + 1) * HEAD] = (
            turned[:, h * tokens : (h + 1) * tokens].T.astype(ref.dtype)
        )


def key_value_copies(all_hbm, kv_ref, width):
    return [
        (all_hbm.at[:, k, :, width + v : width + v + HEAD], kv_ref.at[k, :, :, v : v + HEAD])
        for k in range(2)
        for v in (0, HEAD)
    ]


def keys_of(kv_ref, k):
    value = kv_ref[k, :, :, :HEAD]
    return value.reshape(-1, HEAD)


def values_of(kv_ref, k):
    value = kv_ref[k, :, :, HEAD:]
    return value.reshape(-1, HEAD)


def gradients(k, kv_ref, probs, query, d_att, dout_t, rowdot, kv_grad_refs):
    keys = keys_of(kv_ref, k)
    d_probs = dot(values_of(kv_ref, k), dout_t)
    d_scores = (probs * (d_probs - rowdot)).astype(BF16)
    key_grad = (dot(d_scores, query) * (HEAD ** -0.5)).astype(BF16)
    value_grad = dot(probs.astype(BF16), d_att).astype(BF16)
    tokens = kv_grad_refs[0].shape[1]
    for m in range(keys.shape[0] // tokens):
        rows = slice(m * tokens, (m + 1) * tokens)
        kv_grad_refs[m % 2][m // 2, :, :HEAD] = key_grad[rows]
        kv_grad_refs[m % 2][m // 2, :, HEAD:] = value_grad[rows]
    return dot(keys.astype(F32).T.astype(BF16), d_scores)


def inside(k, tokens, last, opening, dims):
    key = iota(dims, 0) * (2 * tokens) + iota(dims, 1) + k * tokens
    return ((key <= last) & (key >= opening)).reshape(dims[0] * dims[1], dims[2])


def attention_kernel(
    own_ref, lengths_hbm, plan_hbm, all_hbm, dout_hbm,
    out_ref, kv_near_ref, kv_far_ref, stats_ref, bounds_ref, query_ref, query_t, dout_t, query_acc,
    lengths_ref, plan_ref, picked_ref, kv_ref, dout_ref, score_ref, semaphores,
):
    tokens, width = dout_ref.shape
    columns = width // HEAD * tokens
    places = tokens // BLOCK
    half = kv_ref.shape[1] * tokens
    factor = (HEAD ** -0.5) * LOG2E
    tables = begin_copies(((plan_hbm, plan_ref), (lengths_hbm, lengths_ref)), semaphores)
    rest = begin_copies(
        [(dout_hbm.at[0], dout_ref)] + key_value_copies(all_hbm, kv_ref, width),
        semaphores.at[2:7],
    )
    wait_all(tables)
    wanted = [plan_ref[0, own_ref[0] * places + p] for p in range(places)]
    picks = []
    for p, w in enumerate(wanted):
        device, place = lax.div(w, places), lax.rem(w, places)
        rows = pl.ds(pl.multiple_of(place * BLOCK, BLOCK), BLOCK)
        picks.append((
            all_hbm.at[lax.div(device, 2), lax.rem(device, 2), rows, :width],
            picked_ref.at[p * BLOCK : (p + 1) * BLOCK],
        ))
    picks = begin_copies(picks, semaphores.at[7:])

    column = lax.rem(iota((1, columns), 1), tokens)
    place = lax.div(column, BLOCK)
    block = jnp.zeros((1, columns), jnp.int32)
    for p, w in enumerate(wanted):
        block = jnp.where(place == p, w, block)
    last = block * BLOCK + lax.rem(column, BLOCK)
    opening = jnp.zeros((1, columns), jnp.int32)
    for start in starts_of(lengths_ref):
        opening = jnp.where(start <= last, start, opening)
    bounds_ref[:1] = last
    bounds_ref[1:2] = opening

    wait_all(rest[:1])
    d_att = by_head(dout_ref)
    dout_t[...] = d_att.astype(F32).T.astype(BF16)
    wait_all(picks)
    query = by_head(picked_ref)
    query_ref[...] = query
    query_t[...] = query.astype(F32).T.astype(BF16)
    wait_all(rest[1:])

    top = jnp.full((8, columns), NEG, F32)
    for k in range(2):
        scores = dot(keys_of(kv_ref, k), query_t[...])
        dims = (half // tokens, tokens, columns)
        scores = jnp.where(inside(k, tokens, last, opening, dims), scores, NEG)
        score_ref[k] = scores
        top = jnp.maximum(top, jnp.max(scores.reshape(half // 8, 8, columns), axis=0))
    shift = jnp.max(top, axis=0, keepdims=True) * factor

    total = jnp.zeros((8, columns), F32)
    attended = jnp.zeros((HEAD, columns), F32)
    for k in range(2):
        weights = jnp.exp2(score_ref[k] * factor - shift)
        score_ref[k] = weights
        value_t = values_of(kv_ref, k).astype(F32).T.astype(BF16)
        attended = attended + dot(value_t, weights.astype(BF16))
        total = total + jnp.sum(weights.reshape(half // 8, 8, columns), axis=0)
    total = jnp.sum(total, axis=0, keepdims=True)
    inverse = 1.0 / total
    attended = (attended * inverse).astype(BF16).astype(F32)
    turn_back(out_ref, attended)
    rowdot = jnp.sum(attended * dout_t[...].astype(F32), axis=0, keepdims=True)
    stats_ref[:1] = shift + jnp.log(total) * LOG2E
    stats_ref[1:2] = rowdot

    other = 1 - lax.rem(own_ref[0], 2)
    probs = score_ref[other] * inverse
    query_acc[...] = gradients(
        other, kv_ref, probs, query, d_att, dout_t[...], rowdot, (kv_near_ref, kv_far_ref)
    )


def own_half_kernel(
    own_ref, all_hbm, dout_hbm, stats_hbm, bounds_hbm, query_hbm, query_t_hbm, dout_t_hbm, acc_hbm,
    query_grad_ref, kv_near_ref, kv_far_ref,
    kv_ref, dout_ref, stats_ref, bounds_ref, query_ref, query_t, dout_t, query_acc, semaphores,
):
    tokens, width = dout_ref.shape
    half = kv_ref.shape[1] * tokens
    columns = width // HEAD * tokens
    factor = (HEAD ** -0.5) * LOG2E
    own = lax.rem(own_ref[0], 2)
    copies = begin_copies(
        (
            (all_hbm.at[:, own, :, width : width + HEAD], kv_ref.at[0, :, :, :HEAD]),
            (query_t_hbm, query_t), (bounds_hbm, bounds_ref), (stats_hbm, stats_ref),
            (all_hbm.at[:, own, :, width + HEAD :], kv_ref.at[0, :, :, HEAD:]),
            (dout_t_hbm, dout_t), (query_hbm, query_ref), (dout_hbm.at[0], dout_ref),
            (acc_hbm, query_acc),
        ),
        semaphores,
    )
    wait_all(copies)
    scores = dot(keys_of(kv_ref, 0), query_t[...])
    dims = (half // tokens, tokens, columns)
    valid = inside(own, tokens, bounds_ref[:1], bounds_ref[1:2], dims)
    probs = jnp.where(valid, jnp.exp2(scores * factor - stats_ref[:1]), 0.0)
    part = gradients(
        0, kv_ref, probs, query_ref[...], by_head(dout_ref), dout_t[...], stats_ref[1:2],
        (kv_near_ref, kv_far_ref),
    )
    turn_back(query_grad_ref, (query_acc[...] + part) * (HEAD ** -0.5))


VMEM = pl.BlockSpec(memory_space=pltpu.VMEM)
SMEM = pl.BlockSpec(memory_space=pltpu.SMEM)
HBM = pl.BlockSpec(memory_space=pltpu.HBM)
PARAMS = pltpu.CompilerParams(vmem_limit_bytes=63 * 1024 * 1024)


def shape(*dims, dtype=F32):
    return jax.ShapeDtypeStruct(dims, dtype)


def wide(*dims, dtype=F32):
    return pltpu.VMEM(dims, dtype)


def run_summary(own, lengths, x, dt, dy, b, c, a_log, bias):
    tokens, width = x.shape[1:]
    return pl.pallas_call(
        summary_kernel,
        out_shape=(
            shape(SUMMARY_ROWS, width, dtype=BF16),
            shape(NS, SEGS, width), shape(NS, SEGS, width), shape(SEGS, width),
        ),
        in_specs=[SMEM] + [HBM] * 8,
        out_specs=[VMEM] * 4,
        scratch_shapes=[
            pltpu.SMEM(lengths.shape, jnp.int32),
            wide(tokens, width, dtype=BF16), wide(tokens, width, dtype=BF16),
            wide(tokens, width, dtype=BF16),
            wide(NS, tokens, dtype=BF16), wide(NS, tokens, dtype=BF16),
            wide(NS, width), wide(1, width),
            wide(NS, SEGS, width), wide(NS, tokens, LANES), wide(NS, tokens, LANES),
            wide(tokens, width), wide(tokens, width), wide(tokens, width),
            wide(SEGS, width), wide(SEGS, width), wide(2 * NS, SEGS, width),
            pltpu.SemaphoreType.DMA((8,)),
        ],
        compiler_params=PARAMS,
        name="mixer_summary",
    )(own, lengths, x, dt, dy, b, c, a_log, bias)


def run_mixer(own, lengths, x, dt, dy, b, c, a_log, bias, skip, summaries, local):
    tokens, width = x.shape[1:]
    return pl.pallas_call(
        mixer_kernel,
        out_shape=(
            shape(tokens, width, dtype=BF16), shape(tokens, width, dtype=BF16),
            shape(tokens, width, dtype=BF16), shape(2 * NS, tokens), shape(NS + 2, width),
        ),
        in_specs=[SMEM] + [HBM] * 13,
        out_specs=[VMEM] * 5,
        scratch_shapes=[
            pltpu.SMEM(lengths.shape, jnp.int32),
            wide(tokens, width, dtype=BF16), wide(tokens, width, dtype=BF16),
            wide(tokens, width, dtype=BF16),
            wide(NS, tokens, dtype=BF16), wide(NS, tokens, dtype=BF16),
            wide(NS, width), wide(1, width), wide(1, width),
            wide(*summaries.shape, dtype=BF16),
            wide(NS, SEGS, width), wide(NS, SEGS, width), wide(SEGS, width),
            wide(NS, SEGS, width), wide(NS, SEGS, width), wide(NS, SEGS, width),
            wide(NS, tokens, LANES), wide(NS, tokens, LANES),
            wide(tokens, width), wide(tokens, width), wide(tokens, width), wide(tokens, width),
            wide(tokens, width), wide(tokens, width), wide(tokens, width),
            wide(NS, tokens, LANES), wide(NS, tokens, LANES),
            wide(NS, SEGS, width),
            pltpu.SemaphoreType.DMA((13,)),
        ],
        compiler_params=PARAMS,
        name="mixer",
    )(own, lengths, x, dt, dy, b, c, a_log, bias, skip, summaries, *local)


def run_attention(own, lengths, plan, gathered, dout):
    tokens, width = dout.shape[1:]
    pairs = gathered.shape[0]
    columns = width // HEAD * tokens
    kv_shape = shape(pairs // 2, tokens, 2 * HEAD, dtype=BF16)
    out, near, far, *carried = pl.pallas_call(
        attention_kernel,
        out_shape=(
            shape(tokens, width, dtype=BF16), kv_shape, kv_shape,
            shape(8, columns), shape(8, columns, dtype=jnp.int32),
            shape(columns, HEAD, dtype=BF16), shape(HEAD, columns, dtype=BF16),
            shape(HEAD, columns, dtype=BF16), shape(HEAD, columns),
        ),
        in_specs=[SMEM] + [HBM] * 4,
        out_specs=[VMEM] * 9,
        scratch_shapes=[
            pltpu.SMEM(lengths.shape, jnp.int32), pltpu.SMEM(plan.shape, jnp.int32),
            wide(tokens, width, dtype=BF16), wide(2, pairs, tokens, 2 * HEAD, dtype=BF16),
            wide(tokens, width, dtype=BF16), wide(2, pairs * tokens, columns),
            pltpu.SemaphoreType.DMA((7 + tokens // BLOCK,)),
        ],
        compiler_params=PARAMS,
        name="attention",
    )(own, lengths, plan, gathered, dout)
    return out, (near, far), carried


def run_own_half(own, gathered, dout, carried):
    tokens, width = dout.shape[1:]
    pairs = gathered.shape[0]
    columns = width // HEAD * tokens
    kv_shape = shape(pairs // 2, tokens, 2 * HEAD, dtype=BF16)
    query_grad, *kv_parts = pl.pallas_call(
        own_half_kernel,
        out_shape=(shape(tokens, width, dtype=BF16), kv_shape, kv_shape),
        in_specs=[SMEM] + [HBM] * 8,
        out_specs=[VMEM] * 3,
        scratch_shapes=[
            wide(1, pairs, tokens, 2 * HEAD, dtype=BF16), wide(tokens, width, dtype=BF16),
            wide(8, columns), wide(8, columns, dtype=jnp.int32),
            wide(columns, HEAD, dtype=BF16), wide(HEAD, columns, dtype=BF16),
            wide(HEAD, columns, dtype=BF16), wide(HEAD, columns),
            pltpu.SemaphoreType.DMA((9,)),
        ],
        compiler_params=PARAMS,
        name="attention_own_half",
    )(own, gathered, dout, *carried)
    return query_grad, kv_parts


def on_device(
    x_in, dt_in, b_in, c_in, dy_in, a_log, d_skip, dt_bias,
    q_in, k_in, value_input, dout_in, doc_lengths, plan,
):
    seq_count = lax.axis_size("seq")
    own = lax.axis_index("seq").astype(jnp.int32).reshape(1)
    tokens = x_in.shape[1]
    mixer_inputs = (
        own, doc_lengths, x_in, dt_in, dy_in, b_in, c_in, a_log, dt_bias[None],
    )

    mixed = jnp.concatenate([q_in[0], k_in[0], value_input[0]], axis=1)
    gathered = lax.all_gather(mixed, "seq", axis=0, tiled=True)

    summary, *local = run_summary(*mixer_inputs)
    summaries = lax.all_gather(summary, "seq", axis=0)
    output, x_grad, dt_grad, bc_part, params = run_mixer(
        *mixer_inputs, d_skip[None], summaries, local
    )
    one_side = [(i, i ^ 1) for i in range(seq_count)]
    other_side = [(i, (((i + 1) ^ 1) - 1) % seq_count) for i in range(seq_count)]
    same_parity = [
        [*range(k, seq_count, 4), *range(k + 2, seq_count, 4)] for k in range(2)
    ]
    params = params + lax.ppermute(params, "seq", one_side)
    params = jnp.sum(lax.all_gather(params, "dp", axis=0), axis=0)
    gathered, params = lax.optimization_barrier((gathered, params))

    gathered = gathered.reshape(seq_count // 2, 2, tokens, -1)
    attn_out, kv_other, carried = run_attention(own, doc_lengths, plan, gathered, dout_in)
    arrived = [
        lax.ppermute(part, "seq", pairs) for part, pairs in zip(kv_other, (one_side, other_side))
    ]
    query_gradient, kv_own = run_own_half(own, gathered, dout_in, carried)
    kv_pair = [(a.astype(F32) + b.astype(F32)).astype(BF16) for a, b in zip(kv_own, arrived)]
    split = jnp.concatenate([params[:, : 2 * HEAD], params[:, 2 * HEAD :]], 0).astype(BF16)
    spare = -split.shape[0] % 8
    split = jnp.pad(split, ((0, spare), (0, 0)))
    split = jnp.broadcast_to(split[None], (seq_count // 2, *split.shape))
    sent = jnp.concatenate([jnp.concatenate(kv_pair, 0), split], 1)
    sent, bc_part = lax.optimization_barrier((sent, bc_part))
    parts = lax.all_to_all(
        sent, "seq", split_axis=0, concat_axis=0, axis_index_groups=same_parity
    )
    bc_sum = jnp.sum(lax.all_gather(bc_part, "tp", axis=0), axis=0)
    sums = jnp.sum(parts.astype(F32), axis=0)
    kv_sum = sums[:tokens].astype(BF16)
    rows = params.shape[0]
    params_sum = jnp.concatenate(
        [sums[tokens : tokens + rows], sums[tokens + rows : tokens + 2 * rows]], 1
    )
    return (
        output[None],
        x_grad[None],
        dt_grad[None],
        bc_sum[None, :NS],
        bc_sum[None, NS:],
        params_sum[:NS],
        params_sum[NS],
        params_sum[NS + 1],
        attn_out[None],
        query_gradient[None],
        kv_sum[None, :, :HEAD],
        kv_sum[None, :, HEAD:],
    )


def solution(mesh):
    tokens = P("dp", "seq", "tp")
    columns = P("dp", None, "seq")
    row = P("dp", None)
    return jax.shard_map(
        on_device,
        mesh=mesh,
        in_specs=(
            tokens, tokens, columns, columns, tokens, P(None, "tp"), P("tp"), P("tp"),
            tokens, tokens, tokens, tokens, row, row,
        ),
        out_specs=(
            tokens, tokens, tokens, columns, columns, P(None, "tp"), P("tp"), P("tp"),
            tokens, tokens, tokens, tokens,
        ),
        check_vma=False,
    )
```

time: 272 us -> 155 us (0.57)
  the two profiles are of different devices: /device:TPU:32 before, /device:TPU:104 now
where the time goes in v3:
time: 155 us
  blocking collectives  67.5 us (44%)
  waiting for transfers between devices  25.9 us (17%)
  Pallas kernels  22.9 us (15%)
  starting transfers between devices  16.3 us (11%)
  between operations  14.2 us (9%)
  other arithmetic  6.74 us (4%)
    all_gather x1, blocking collectives, on_device(): summaries = lax.all_gather(summary, 'seq', axis=0)  43 us
    all_to_all x1, waiting for transfers between devices, on_device(): lax.all_to_all(sent, 'seq', split_axis=0, concat_axis=0, axis_index_group...  15.8 us
    all_gather x1, blocking collectives, on_device(): params = jnp.sum(lax.all_gather(params, 'dp', axis=0), axis=0)  12.4 us
    all_gather x1, blocking collectives, on_device(): bc_sum = jnp.sum(lax.all_gather(bc_part, 'tp', axis=0), axis=0)  12.1 us
    pallas_call x1, Pallas kernels, run_mixer(): pl.pallas_call(mixer_kernel, out_shape=(shape(tokens, width, dtype=BF16),...  8.01 us
    all_to_all x1, starting transfers between devices, on_device(): lax.all_to_all(sent, 'seq', split_axis=0, concat_axis=0, axis_index_group...  7.87 us
    ppermute x2, starting transfers between devices, on_device(): lax.ppermute(part, 'seq', pairs)  6.51 us
    pallas_call x1, Pallas kernels, run_attention(): pl.pallas_call(attention_kernel, out_shape=(shape(tokens, width, dtype=BF...  5.68 us
  transfers between devices with their start and end apart: 5, of which 4 were waited for; matrix products, arithmetic and copies ran while one was open for 2% of the time, Pallas kernels for 11%

profile of v3, /device:TPU:104, one launch (start us, length us, event | category | flops | bytes accessed | tf_op | source)
XLA Modules:
  0.0 154.8 jit_solution(11905363949470496963)
XLA Ops:
  7.2 0.0 all-gather.6.cloned.1.call-start
  7.2 1.7 %pad_maximum_fusion.1 = bf16[128,768]{1,0:T(8,128)(2,1)} fusion(bf16[128,128]{1,0:T(8,128)(2,1)} %bitcast.31, bf16[128,128]{1,0:T(8,128)(2,1)} %bitcast.32, bf16[128,512]{1,0:T(8,128)(2,1)} %bitcast.30), kind=kLoop, calls=%fused_computation.4 | loop fusion | flops 589824 | bytes 393216 | tf_op jit(solution)/shard_map/concatenate | solution.py:633
  8.9 0.0 all-gather.6.cloned.1.call-update
  8.9 5.2 %mixer_summary.1 = (bf16[48,512]{1,0:T(8,128)(2,1)}, f32[16,8,512]{2,1,0:T(8,128)}, f32[16,8,512]{2,1,0:T(8,128)}, f32[8,512]{1,0:T(8,128)}) custom-call(s32[1]{0:T(128)} %bitcast.own_ref, s32[1,8]{1,0:T(1,128)} %lengths_hbm.5, bf16[1,128,512]{2,1,0:T(8,128)(2,1)} %x_hbm.3, bf16[1,128,512]{2,1,0:T(8,128)(2,1)} %dt_hbm.3, bf16[1,128,512]{2,1,0:T(8,128)(2,1)} %dy_hbm.3, ...), custom_call_target="tpu_custom_call" | custom-call | tf_op jit(solution)/shard_map/mixer_summary/pallas_call | solution.py:517
  14.1 43.0 %all-gather = bf16[768,512]{1,0:T(8,128)(2,1)} all-gather(bf16[48,512]{1,0:T(8,128)(2,1)} %get-tuple-element.37), channel_id=2, replica_groups=mesh['seq'=16,'tp'=8,'dp'=4] {'seq'}, dimensions={0}, use_global_device_ids=true | all-gather | bytes 835584 | tf_op jit(solution)/shard_map/all_gather | solution.py:637
  57.2 8.0 %mixer.1 = (bf16[128,512]{1,0:T(8,128)(2,1)}, bf16[128,512]{1,0:T(8,128)(2,1)}, bf16[128,512]{1,0:T(8,128)(2,1)}, f32[32,128]{1,0:T(8,128)}, f32[18,512]{1,0:T(8,128)}) custom-call(s32[1]{0:T(128)} %bitcast.own_ref, s32[1,8]{1,0:T(1,128)} %lengths_hbm.5, bf16[1,128,512]{2,1,0:T(8,128)(2,1)} %x_hbm.3, bf16[1,128,512]{2,1,0:T(8,128)(2,1)} %dt_hbm.3, ...), custom_call_target="tpu_custom_call" | custom-call | tf_op jit(solution)/shard_map/mixer/pallas_call | solution.py:543
  65.2 1.9 %collective-permute-start = (f32[18,512]{1,0:T(8,128)}, f32[18,512]{1,0:T(8,128)S(1)}, u32[]{:S(2)}, u32[]{:S(2)}) collective-permute-start(f32[18,512]{1,0:T(8,128)} %get-tuple-element.44), channel_id=1, source_target_pairs={{0,32},{32,0},{64,96},{96,64},{128,160},{160,128},{192,224},{224,1... | collective-permute-start | bytes 110600 | tf_op jit(solution)/shard_map/ppermute | solution.py:646
  67.1 5.0 %collective-permute-done = f32[18,512]{1,0:T(8,128)S(1)} collective-permute-done((f32[18,512]{1,0:T(8,128)}, f32[18,512]{1,0:T(8,128)S(1)}, u32[]{:S(2)}, u32[]{:S(2)}) %collective-permute-start) | collective-permute-done | bytes 36896 | tf_op jit(solution)/shard_map/ppermute | solution.py:646
  72.1 0.8 add_bitcast_fusion
  72.9 12.4 %all-gather.3 = f32[4,18,512]{2,1,0:T(8,128)S(1)} all-gather(f32[1,18,512]{2,1,0:T(8,128)S(1)} %add_bitcast_fusion), channel_id=3, replica_groups=mesh['seq'=16,'tp'=8,'dp'=4] {'dp'}, dimensions={0}, use_global_device_ids=true | all-gather | bytes 184320 | tf_op jit(solution)/shard_map/all_gather | solution.py:647
  85.3 4.5 %all-gather.6.cloned.1.call-done = bf16[2048,768]{1,0:T(8,128)(2,1)} async-done(((bf16[128,768]{1,0:T(8,128)(2,1)}), bf16[2048,768]{1,0:T(8,128)(2,1)}) %all-gather.6.cloned.1.call-update) | async-done | bytes 3145744 | tf_op jit(solution)/shard_map/all_gather | solution.py:634
  89.8 5.7 %attention.1 = (bf16[128,512]{1,0:T(8,128)(2,1)}, bf16[4,128,256]{2,1,0:T(8,128)(2,1)}, bf16[4,128,256]{2,1,0:T(8,128)(2,1)}, f32[8,512]{1,0:T(8,128)}, s32[8,51...) custom-call(s32[1]{0:T(128)} %bitcast.own_ref, ...), custom_call_target="tpu_custom_call" | custom-call | tf_op jit(solution)/shard_map/attention/pallas_call | solution.py:577
  95.5 2.4 %collective-permute-start.1 = (bf16[4,128,256]{2,1,0:T(8,128)(2,1)}, bf16[4,128,256]{2,1,0:T(8,128)(2,1)S(1)}, u32[]{:S(2)}, u32[]{:S(2)}) collective-permute-start(bf16[4,128,256]{2,1,0:T(8,128)(2,1)} %get-tuple-element.53), channel_id=1, source_target_pairs={{0,32},{32,0},{64,96},{96,64},{128,160},{160,128},{192,224},{224,1... | collective-permute-start | bytes 786440 | tf_op jit(solution)/shard_map/ppermute | solution.py:653
  98.0 4.1 %collective-permute-start.2 = (bf16[4,128,256]{2,1,0:T(8,128)(2,1)}, bf16[4,128,256]{2,1,0:T(8,128)(2,1)S(1)}, u32[]{:S(2)}, u32[]{:S(2)}) collective-permute-start(bf16[4,128,256]{2,1,0:T(8,128)(2,1)} %get-tuple-element.55), channel_id=1, source_target_pairs={{0,480},{32,64},{64,32},{96,128},{128,96},{160,192},{192,160},{224... | collective-permute-start | bytes 786440 | tf_op jit(solution)/shard_map/ppermute | solution.py:653
  102.1 3.9 %attention_own_half.1 = (bf16[128,512]{1,0:T(8,128)(2,1)}, bf16[4,128,256]{2,1,0:T(8,128)(2,1)}, bf16[4,128,256]{2,1,0:T(8,128)(2,1)}) custom-call(s32[1]{0:T(128)} %bitcast.own_ref, bf16[8,2,128,768]{3,2,1,0:T(8,128)(2,1)} %bitcast.27, bf16[1,128,512]{2,1,0:T(8,128)(2,1)} %dout_hbm.3, f32[8,512]{1,0:T(8,128)} %get-tuple-element.46.stats_hbm, ...), custom_call_target="tpu_custom_call" | custom-call | tf_op jit(solution)/shard_map/attention_own_half/pallas_call | solution.py:604
  106.0 0.0 collective-permute-done.1
  106.0 1.0 add_convert_fusion.1
  107.0 0.6 collective-permute-done.2
  107.6 1.0 add_convert_fusion
  108.7 0.0 copy-start
  108.7 0.9 pad_maximum_fusion
  109.6 7.9 %all-to-all-start = ((bf16[8,168,256]{2,1,0:T(8,128)(2,1)}), bf16[8,168,256]{2,1,0:T(8,128)(2,1)S(1)}, u32[]{:S(2)}, u32[]{:S(2)}) async-start(bf16[8,168,256]{2,1,0:T(8,128)(2,1)} %pad_maximum_fusion), calls=%async_computation | async-start | bytes 1376256 | tf_op jit(solution)/shard_map/all_to_all | solution.py:663
  117.5 0.0 copy-done
  117.5 12.1 %all-gather.2 = f32[256,128]{1,0:T(8,128)S(1)} all-gather(f32[32,128]{1,0:T(8,128)S(1)} %copy-done), channel_id=4, replica_groups=mesh['seq'=16,'tp'=8,'dp'=4] {'tp'}, dimensions={0}, use_global_device_ids=true | all-gather | bytes 147456 | tf_op jit(solution)/shard_map/all_gather | solution.py:666
  129.6 0.6 slice_bitcast_fusion.2
  130.2 15.8 %all-to-all-done = bf16[8,168,256]{2,1,0:T(8,128)(2,1)S(1)} async-done(((bf16[8,168,256]{2,1,0:T(8,128)(2,1)}), bf16[8,168,256]{2,1,0:T(8,128)(2,1)S(1)}, u32[]{:S(2)}, u32[]{:S(2)}) %all-to-all-start) | async-done | bytes 688160 | tf_op jit(solution)/shard_map/all_to_all | solution.py:663
  146.0 0.1 convert_reduce_fusion
  146.1 0.6 pad_maximum_fusion.2
  146.7 0.6 fusion.2
  147.4 0.6 slice_bitcast_fusion
  (7 shorter events, 0.1 us)
Async XLA Ops:
  7.2 82.6 %all-gather.6.cloned.1.call-start = ((), (), s32[]{:S(2)}) async-start(), calls=%async_computation.1 | async-start | bytes 3342336 | tf_op jit(solution)/shard_map/all_gather | solution.py:634
  65.2 6.9 %collective-permute-start = (f32[18,512]{1,0:T(8,128)}, f32[18,512]{1,0:T(8,128)S(1)}, u32[]{:S(2)}, u32[]{:S(2)}) collective-permute-start(f32[18,512]{1,0:T(8,128)} %get-tuple-element.44), channel_id=1, source_target_pairs={{0,32},{32,0},{64,96},{96,64},{128,160},{160,128},{192,224},{224,1... | collective-permute-start | bytes 110600 | tf_op jit(solution)/shard_map/ppermute | solution.py:646
  95.5 10.5 %collective-permute-start.1 = (bf16[4,128,256]{2,1,0:T(8,128)(2,1)}, bf16[4,128,256]{2,1,0:T(8,128)(2,1)S(1)}, u32[]{:S(2)}, u32[]{:S(2)}) collective-permute-start(bf16[4,128,256]{2,1,0:T(8,128)(2,1)} %get-tuple-element.53), channel_id=1, source_target_pairs={{0,32},{32,0},{64,96},{96,64},{128,160},{160,128},{192,224},{224,1... | collective-permute-start | bytes 786440 | tf_op jit(solution)/shard_map/ppermute | solution.py:653
  98.0 9.7 %collective-permute-start.2 = (bf16[4,128,256]{2,1,0:T(8,128)(2,1)}, bf16[4,128,256]{2,1,0:T(8,128)(2,1)S(1)}, u32[]{:S(2)}, u32[]{:S(2)}) collective-permute-start(bf16[4,128,256]{2,1,0:T(8,128)(2,1)} %get-tuple-element.55), channel_id=1, source_target_pairs={{0,480},{32,64},{64,32},{96,128},{128,96},{160,192},{192,160},{224... | collective-permute-start | bytes 786440 | tf_op jit(solution)/shard_map/ppermute | solution.py:653
  108.7 8.8 %copy-start = (f32[32,128]{1,0:T(8,128)S(1)}, f32[32,128]{1,0:T(8,128)}, u32[]{:S(2)}) copy-start(f32[32,128]{1,0:T(8,128)} %get-tuple-element.58) | copy-start | bytes 49156
  109.6 36.4 %all-to-all-start = ((bf16[8,168,256]{2,1,0:T(8,128)(2,1)}), bf16[8,168,256]{2,1,0:T(8,128)(2,1)S(1)}, u32[]{:S(2)}, u32[]{:S(2)}) async-start(bf16[8,168,256]{2,1,0:T(8,128)(2,1)} %pad_maximum_fusion), calls=%async_computation | async-start | bytes 1376256 | tf_op jit(solution)/shard_map/all_to_all | solution.py:663
Sparse Core Ops, SparseCore 0:
  10.1 79.6 all-gather.5

commit v4 on v3

--- a/solution.py
+++ b/solution.py
@@ -13,7 +13,6 @@
 RESET = 1e30
 LOG2E = 1.4426950408889634
 NEG = -1e30
-SUMMARY_ROWS = 48
 
 F32 = jnp.float32
 BF16 = jnp.bfloat16
@@ -147,11 +146,10 @@
     after_ref[...] = after
     before_ref[...] = before
     whole = before[SEGS - 1 :] + total[SEGS - 1 :]
-    high = whole.astype(BF16)
-    low = (whole - high.astype(F32)).astype(BF16)
-    summary_ref[2 * NS :] = jnp.zeros((SUMMARY_ROWS - 2 * NS, width), BF16)
-    summary_ref[2 * NS : 2 * NS + 1] = high
-    summary_ref[2 * NS + 1 : 2 * NS + 2] = low
+    high = whole.astype(BF16).astype(F32)
+    low = whole - high
+    ends = [part[:, lane : lane + LANES] for part in (high, low) for lane in range(0, width, LANES)]
+    summary_ref[2 * NS * width // LANES :] = jnp.concatenate(ends, 0).astype(BF16)
 
     def state_row(n, carry):
         state_rows, adjoint_rows = [], []
@@ -187,7 +185,9 @@
 
     lax.fori_loop(0, NS, state_row, 0)
     gathered = jnp.concatenate([rows_ref[n, :1] for n in range(2 * NS)], 0)
-    summary_ref[: 2 * NS] = gathered.astype(BF16)
+    for k in range(width // LANES):
+        rows = slice(2 * NS * k, 2 * NS * (k + 1))
+        summary_ref[rows] = gathered[:, k * LANES : (k + 1) * LANES].astype(BF16)
 
 
 def mixer_kernel(
@@ -231,15 +231,22 @@
     entering = jnp.zeros((NS, width), F32)
     arriving = jnp.zeros((NS, width), F32)
 
+    groups = width // LANES
+
     def factor(j):
-        ends = summaries_ref[j, 2 * NS : 2 * NS + 2].astype(F32)
-        return jnp.exp2(rate2_all * (ends[0:1] + ends[1:2]))
+        ends = summaries_ref[j, 2 * NS * groups :].astype(F32)
+        ends = ends[:groups] + ends[groups:]
+        return jnp.exp2(rate2_all * jnp.concatenate([ends[k : k + 1] for k in range(groups)], 1))
+
+    def summed(j, first):
+        starts = range(first, 2 * NS * groups, 2 * NS)
+        return jnp.concatenate([summaries_ref[j, k : k + NS].astype(F32) for k in starts], 1)
 
     for j in range(count - 1):
-        longer = factor(j) * entering + summaries_ref[j, :NS].astype(F32)
+        longer = factor(j) * entering + summed(j, 0)
         entering = jnp.where(j < own, longer, entering)
     for j in reversed(range(1, count)):
-        longer = factor(j) * arriving + summaries_ref[j, NS : 2 * NS].astype(F32)
+        longer = factor(j) * arriving + summed(j, NS)
         arriving = jnp.where(j > own, longer, arriving)
     spread(entering, enter_ref)
     spread(arriving, arrive_ref)
@@ -387,21 +394,15 @@
 
 
 def attention_kernel(
-    own_ref, lengths_hbm, plan_hbm, all_hbm, dout_hbm,
+    own_ref, lengths_ref, plan_ref, all_hbm, dout_hbm,
     out_ref, kv_near_ref, kv_far_ref, stats_ref, bounds_ref, query_ref, query_t, dout_t, query_acc,
-    lengths_ref, plan_ref, picked_ref, kv_ref, dout_ref, score_ref, semaphores,
+    picked_ref, kv_ref, dout_ref, score_ref, semaphores,
 ):
     tokens, width = dout_ref.shape
     columns = width // HEAD * tokens
     places = tokens // BLOCK
     half = kv_ref.shape[1] * tokens
     factor = (HEAD ** -0.5) * LOG2E
-    tables = begin_copies(((plan_hbm, plan_ref), (lengths_hbm, lengths_ref)), semaphores)
-    rest = begin_copies(
-        [(dout_hbm.at[0], dout_ref)] + key_value_copies(all_hbm, kv_ref, width),
-        semaphores.at[2:7],
-    )
-    wait_all(tables)
     wanted = [plan_ref[0, own_ref[0] * places + p] for p in range(places)]
     picks = []
     for p, w in enumerate(wanted):
@@ -411,7 +412,10 @@
             all_hbm.at[lax.div(device, 2), lax.rem(device, 2), rows, :width],
             picked_ref.at[p * BLOCK : (p + 1) * BLOCK],
         ))
-    picks = begin_copies(picks, semaphores.at[7:])
+    picks = begin_copies(picks, semaphores.at[5:])
+    rest = begin_copies(
+        [(dout_hbm.at[0], dout_ref)] + key_value_copies(all_hbm, kv_ref, width), semaphores
+    )
 
     column = lax.rem(iota((1, columns), 1), tokens)
     place = lax.div(column, BLOCK)
@@ -445,9 +449,9 @@
 
     total = jnp.zeros((8, columns), F32)
     attended = jnp.zeros((HEAD, columns), F32)
-    for k in range(2):
+    other = 1 - lax.rem(own_ref[0], 2)
+    for k in (1 - other, other):
         weights = jnp.exp2(score_ref[k] * factor - shift)
-        score_ref[k] = weights
         value_t = values_of(kv_ref, k).astype(F32).T.astype(BF16)
         attended = attended + dot(value_t, weights.astype(BF16))
         total = total + jnp.sum(weights.reshape(half // 8, 8, columns), axis=0)
@@ -459,8 +463,7 @@
     stats_ref[:1] = shift + jnp.log(total) * LOG2E
     stats_ref[1:2] = rowdot
 
-    other = 1 - lax.rem(own_ref[0], 2)
-    probs = score_ref[other] * inverse
+    probs = weights * inverse
     query_acc[...] = gradients(
         other, kv_ref, probs, query, d_att, dout_t[...], rowdot, (kv_near_ref, kv_far_ref)
     )
@@ -486,11 +489,12 @@
         ),
         semaphores,
     )
-    wait_all(copies)
+    wait_all(copies[:4])
     scores = dot(keys_of(kv_ref, 0), query_t[...])
     dims = (half // tokens, tokens, columns)
     valid = inside(own, tokens, bounds_ref[:1], bounds_ref[1:2], dims)
     probs = jnp.where(valid, jnp.exp2(scores * factor - stats_ref[:1]), 0.0)
+    wait_all(copies[4:])
     part = gradients(
         0, kv_ref, probs, query_ref[...], by_head(dout_ref), dout_t[...], stats_ref[1:2],
         (kv_near_ref, kv_far_ref),
@@ -517,7 +521,7 @@
     return pl.pallas_call(
         summary_kernel,
         out_shape=(
-            shape(SUMMARY_ROWS, width, dtype=BF16),
+            shape(2 * (NS + 1) * width // LANES, LANES, dtype=BF16),
             shape(NS, SEGS, width), shape(NS, SEGS, width), shape(SEGS, width),
         ),
         in_specs=[SMEM] + [HBM] * 8,
@@ -582,15 +586,18 @@
             shape(columns, HEAD, dtype=BF16), shape(HEAD, columns, dtype=BF16),
             shape(HEAD, columns, dtype=BF16), shape(HEAD, columns),
         ),
-        in_specs=[SMEM] + [HBM] * 4,
+        in_specs=[SMEM] * 3 + [HBM] * 2,
         out_specs=[VMEM] * 9,
         scratch_shapes=[
-            pltpu.SMEM(lengths.shape, jnp.int32), pltpu.SMEM(plan.shape, jnp.int32),
             wide(tokens, width, dtype=BF16), wide(2, pairs, tokens, 2 * HEAD, dtype=BF16),
             wide(tokens, width, dtype=BF16), wide(2, pairs * tokens, columns),
-            pltpu.SemaphoreType.DMA((7 + tokens // BLOCK,)),
+            pltpu.SemaphoreType.DMA((5 + tokens // BLOCK,)),
         ],
         compiler_params=PARAMS,
+        cost_estimate=pl.CostEstimate(
+            flops=10 * pairs * tokens * columns * HEAD, bytes_accessed=8 * gathered.size,
+            transcendentals=2 * pairs * tokens * columns,
+        ),
         name="attention",
     )(own, lengths, plan, gathered, dout)
     return out, (near, far), carried
@@ -614,6 +621,10 @@
             pltpu.SemaphoreType.DMA((9,)),
         ],
         compiler_params=PARAMS,
+        cost_estimate=pl.CostEstimate(
+            flops=8 * pairs * tokens * columns * HEAD, bytes_accessed=4 * gathered.size,
+            transcendentals=pairs * tokens * columns,
+        ),
         name="attention_own_half",
     )(own, gathered, dout, *carried)
     return query_grad, kv_parts
@@ -645,7 +656,16 @@
     ]
     params = params + lax.ppermute(params, "seq", one_side)
     params = jnp.sum(lax.all_gather(params, "dp", axis=0), axis=0)
-    gathered, params = lax.optimization_barrier((gathered, params))
+    rows = params.shape[0] // 2
+    first = lax.rem(own[0], 4) < 2
+    theirs = lax.ppermute(
+        jnp.where(first, params[rows:], params[:rows]),
+        "seq", [(i, i ^ 2) for i in range(seq_count)],
+    )
+    params = jnp.where(first, params[:rows], params[rows:]) + theirs
+    split = jnp.concatenate([params[:, : 2 * HEAD], params[:, 2 * HEAD :]], 0).astype(BF16)
+    split = jnp.pad(split, ((0, -2 * rows % 8), (0, 0)))
+    gathered, split = lax.optimization_barrier((gathered, split))
 
     gathered = gathered.reshape(seq_count // 2, 2, tokens, -1)
     attn_out, kv_other, carried = run_attention(own, doc_lengths, plan, gathered, dout_in)
@@ -654,9 +674,6 @@
     ]
     query_gradient, kv_own = run_own_half(own, gathered, dout_in, carried)
     kv_pair = [(a.astype(F32) + b.astype(F32)).astype(BF16) for a, b in zip(kv_own, arrived)]
-    split = jnp.concatenate([params[:, : 2 * HEAD], params[:, 2 * HEAD :]], 0).astype(BF16)
-    spare = -split.shape[0] % 8
-    split = jnp.pad(split, ((0, spare), (0, 0)))
     split = jnp.broadcast_to(split[None], (seq_count // 2, *split.shape))
     sent = jnp.concatenate([jnp.concatenate(kv_pair, 0), split], 1)
     sent, bc_part = lax.optimization_barrier((sent, bc_part))
@@ -664,12 +681,10 @@
         sent, "seq", split_axis=0, concat_axis=0, axis_index_groups=same_parity
     )
     bc_sum = jnp.sum(lax.all_gather(bc_part, "tp", axis=0), axis=0)
-    sums = jnp.sum(parts.astype(F32), axis=0)
-    kv_sum = sums[:tokens].astype(BF16)
-    rows = params.shape[0]
-    params_sum = jnp.concatenate(
-        [sums[tokens : tokens + rows], sums[tokens + rows : tokens + 2 * rows]], 1
-    )
+    kv_sum = jnp.sum(parts[:, :tokens].astype(F32), axis=0).astype(BF16)
+    params_sum = parts[:, tokens : tokens + 2 * rows].astype(F32)
+    params_sum = jnp.sum(params_sum.reshape(2, seq_count // 4, 2, rows, 2 * HEAD), axis=1)
+    params_sum = jnp.concatenate([params_sum[:, 0], params_sum[:, 1]], 2).reshape(2 * rows, -1)
     return (
         output[None],
         x_grad[None],

time: 155 us -> 152 us (0.981)
  the two profiles are of different devices: /device:TPU:104 before, /device:TPU:98 now
where the time goes in v4:
time: 152 us
  blocking collectives  62.8 us (41%)
  Pallas kernels  22.9 us (15%)
  waiting for transfers between devices  22.1 us (15%)
  starting transfers between devices  21.8 us (14%)
  between operations  14.2 us (9%)
  other arithmetic  5.49 us (4%)
  local copies, waits for them, and re-layouts  2.51 us (2%)
    all_gather x1, blocking collectives, on_device(): summaries = lax.all_gather(summary, 'seq', axis=0)  37.8 us
    all_gather x1, blocking collectives, on_device(): bc_sum = jnp.sum(lax.all_gather(bc_part, 'tp', axis=0), axis=0)  13 us
    all_gather x1, blocking collectives, on_device(): params = jnp.sum(lax.all_gather(params, 'dp', axis=0), axis=0)  12.1 us
    all_to_all x1, waiting for transfers between devices, on_device(): lax.all_to_all(sent, 'seq', split_axis=0, concat_axis=0, axis_index_group...  11.6 us
    pallas_call x1, Pallas kernels, run_mixer(): pl.pallas_call(mixer_kernel, out_shape=(shape(tokens, width, dtype=BF16),...  7.9 us
    all_to_all x1, starting transfers between devices, on_device(): lax.all_to_all(sent, 'seq', split_axis=0, concat_axis=0, axis_index_group...  7.28 us
    pallas_call x1, Pallas kernels, run_attention(): pl.pallas_call(attention_kernel, out_shape=(shape(tokens, width, dtype=BF...  5.89 us
    ppermute x2, starting transfers between devices, on_device(): lax.ppermute(part, 'seq', pairs)  5.85 us
  transfers between devices with their start and end apart: 6, of which 5 were waited for; matrix products, arithmetic and copies ran while one was open for 2% of the time, Pallas kernels for 11%

profile of v4, /device:TPU:98, one launch (start us, length us, event | category | flops | bytes accessed | tf_op | source)
XLA Modules:
  0.0 151.9 jit_solution(17054964683178342731)
XLA Ops:
  7.2 0.0 all-gather.6.cloned.1.call-start
  7.2 1.6 %pad_maximum_fusion.1 = bf16[128,768]{1,0:T(8,128)(2,1)} fusion(bf16[128,128]{1,0:T(8,128)(2,1)} %bitcast.40, bf16[128,128]{1,0:T(8,128)(2,1)} %bitcast.41, bf16[128,512]{1,0:T(8,128)(2,1)} %bitcast.39), kind=kLoop, calls=%fused_computation.4 | loop fusion | flops 589824 | bytes 393216 | tf_op jit(solution)/shard_map/concatenate | solution.py:644
  8.9 0.0 all-gather.6.cloned.1.call-update
  8.9 5.3 %mixer_summary.1 = (bf16[136,128]{1,0:T(8,128)(2,1)}, f32[16,8,512]{2,1,0:T(8,128)}, f32[16,8,512]{2,1,0:T(8,128)}, f32[8,512]{1,0:T(8,128)}) custom-call(s32[1]{0:T(128)} %bitcast.own_ref, s32[1,8]{1,0:T(1,128)} %lengths_ref.1, bf16[1,128,512]{2,1,0:T(8,128)(2,1)} %x_hbm.3, bf16[1,128,512]{2,1,0:T(8,128)(2,1)} %dt_hbm.3, bf16[1,128,512]{2,1,0:T(8,128)(2,1)} %dy_hbm.3, ...), custom_call_target="tpu_custom_call" | custom-call | tf_op jit(solution)/shard_map/mixer_summary/pallas_call | solution.py:521
  14.2 37.8 %all-gather = bf16[2176,128]{1,0:T(8,128)(2,1)} all-gather(bf16[136,128]{1,0:T(8,128)(2,1)} %get-tuple-element.37), channel_id=2, replica_groups=mesh['seq'=16,'tp'=8,'dp'=4] {'seq'}, dimensions={0}, use_global_device_ids=true | all-gather | bytes 591872 | tf_op jit(solution)/shard_map/all_gather | solution.py:648
  51.9 7.9 %mixer.1 = (bf16[128,512]{1,0:T(8,128)(2,1)}, bf16[128,512]{1,0:T(8,128)(2,1)}, bf16[128,512]{1,0:T(8,128)(2,1)}, f32[32,128]{1,0:T(8,128)}, f32[18,512]{1,0:T(8,128)}) custom-call(s32[1]{0:T(128)} %bitcast.own_ref, s32[1,8]{1,0:T(1,128)} %lengths_ref.1, bf16[1,128,512]{2,1,0:T(8,128)(2,1)} %x_hbm.3, bf16[1,128,512]{2,1,0:T(8,128)(2,1)} %dt_hbm.3, ...), custom_call_target="tpu_custom_call" | custom-call | tf_op jit(solution)/shard_map/mixer/pallas_call | solution.py:547
  59.9 4.2 %collective-permute-start = (f32[18,512]{1,0:T(8,128)}, f32[18,512]{1,0:T(8,128)S(1)}, u32[]{:S(2)}, u32[]{:S(2)}) collective-permute-start(f32[18,512]{1,0:T(8,128)} %get-tuple-element.44), channel_id=1, source_target_pairs={{0,32},{32,0},{64,96},{96,64},{128,160},{160,128},{192,224},{224,1... | collective-permute-start | bytes 110600 | tf_op jit(solution)/shard_map/ppermute | solution.py:657
  64.0 2.9 %collective-permute-done = f32[18,512]{1,0:T(8,128)S(1)} collective-permute-done((f32[18,512]{1,0:T(8,128)}, f32[18,512]{1,0:T(8,128)S(1)}, u32[]{:S(2)}, u32[]{:S(2)}) %collective-permute-start) | collective-permute-done | bytes 36896 | tf_op jit(solution)/shard_map/ppermute | solution.py:657
  66.9 0.8 add_bitcast_fusion
  67.7 12.1 %all-gather.3 = f32[4,18,512]{2,1,0:T(8,128)S(1)} all-gather(f32[1,18,512]{2,1,0:T(8,128)S(1)} %add_bitcast_fusion), channel_id=3, replica_groups=mesh['seq'=16,'tp'=8,'dp'=4] {'dp'}, dimensions={0}, use_global_device_ids=true | all-gather | bytes 184320 | tf_op jit(solution)/shard_map/all_gather | solution.py:658
  79.9 4.5 %collective-permute-start.1 = (f32[9,512]{1,0:T(8,128)S(1)}, f32[9,512]{1,0:T(8,128)S(1)}, u32[]{:S(2)}, u32[]{:S(2)}) collective-permute-start(f32[9,512]{1,0:T(8,128)S(1)} %slice_select_fusion), channel_id=1, source_target_pairs={{0,64},{32,96},{64,0},{96,32},{128,192},{160,224},{192,128},{224,1... | collective-permute-start | bytes 55304 | tf_op jit(solution)/shard_map/ppermute | solution.py:661
  84.3 2.2 %collective-permute-done.1 = f32[9,512]{1,0:T(8,128)S(1)} collective-permute-done((f32[9,512]{1,0:T(8,128)S(1)}, f32[9,512]{1,0:T(8,128)S(1)}, u32[]{:S(2)}, u32[]{:S(2)}) %collective-permute-start.1) | collective-permute-done | bytes 18464 | tf_op jit(solution)/shard_map/ppermute | solution.py:661
  86.6 4.4 %all-gather.6.cloned.1.call-done = bf16[2048,768]{1,0:T(8,128)(2,1)} async-done(((bf16[128,768]{1,0:T(8,128)(2,1)}), bf16[2048,768]{1,0:T(8,128)(2,1)}) %all-gather.6.cloned.1.call-update) | async-done | bytes 3145744 | tf_op jit(solution)/shard_map/all_gather | solution.py:645
  91.1 5.9 %attention.1 = (bf16[128,512]{1,0:T(8,128)(2,1)}, bf16[4,128,256]{2,1,0:T(8,128)(2,1)}, bf16[4,128,256]{2,1,0:T(8,128)(2,1)}, f32[8,512]{1,0:T(8,128)}, s32[8,51...) custom-call(s32[1]{0:T(128)} %bitcast.own_ref, ...), custom_call_target="tpu_custom_call" | custom-call | flops 671088640 | bytes 12582912 | tf_op jit(solution)/shard_map/attention/pallas_call | solution.py:581
  97.0 1.9 %collective-permute-start.2 = (bf16[4,128,256]{2,1,0:T(8,128)(2,1)}, bf16[4,128,256]{2,1,0:T(8,128)(2,1)S(1)}, u32[]{:S(2)}, u32[]{:S(2)}) collective-permute-start(bf16[4,128,256]{2,1,0:T(8,128)(2,1)} %get-tuple-element.53), channel_id=1, source_target_pairs={{0,32},{32,0},{64,96},{96,64},{128,160},{160,128},{192,224},{224,1... | collective-permute-start | bytes 786440 | tf_op jit(solution)/shard_map/ppermute | solution.py:673
  98.9 3.9 %collective-permute-start.3 = (bf16[4,128,256]{2,1,0:T(8,128)(2,1)}, bf16[4,128,256]{2,1,0:T(8,128)(2,1)S(1)}, u32[]{:S(2)}, u32[]{:S(2)}) collective-permute-start(bf16[4,128,256]{2,1,0:T(8,128)(2,1)} %get-tuple-element.55), channel_id=1, source_target_pairs={{0,480},{32,64},{64,32},{96,128},{128,96},{160,192},{192,160},{224... | collective-permute-start | bytes 786440 | tf_op jit(solution)/shard_map/ppermute | solution.py:673
  102.8 3.8 %attention_own_half.1 = (bf16[128,512]{1,0:T(8,128)(2,1)}, bf16[4,128,256]{2,1,0:T(8,128)(2,1)}, bf16[4,128,256]{2,1,0:T(8,128)(2,1)}) custom-call(s32[1]{0:T(128)} %bitcast.own_ref, bf16[8,2,128,768]{3,2,1,0:T(8,128)(2,1)} %bitcast.35, bf16[1,128,512]{2,1,0:T(8,128)(2,1)} %dout_hbm.3, f32[8,512]{1,0:T(8,128)} %get-tuple-element.46.stats_hbm, ...), custom_call_target="tpu_custom_call" | custom-call | flops 536870912 | bytes 6291456 | tf_op jit(solution)/shard_map/attention_own_half/pallas_call | solution.py:611
  106.7 0.0 collective-permute-done.2
  106.7 1.0 add_convert_fusion.1
  107.7 0.9 collective-permute-done.3
  108.6 1.0 add_convert_fusion
  109.6 0.0 copy-start
  109.6 0.9 pad_maximum_fusion
  110.5 7.3 %all-to-all-start = ((bf16[8,152,256]{2,1,0:T(8,128)(2,1)}), bf16[8,152,256]{2,1,0:T(8,128)(2,1)S(1)}, u32[]{:S(2)}, u32[]{:S(2)}) async-start(bf16[8,152,256]{2,1,0:T(8,128)(2,1)} %pad_maximum_fusion), calls=%async_computation | async-start | bytes 1245184 | tf_op jit(solution)/shard_map/all_to_all | solution.py:680
  117.8 0.0 copy-done
  117.8 13.0 %all-gather.2 = f32[256,128]{1,0:T(8,128)S(1)} all-gather(f32[32,128]{1,0:T(8,128)S(1)} %copy-done), channel_id=4, replica_groups=mesh['seq'=16,'tp'=8,'dp'=4] {'tp'}, dimensions={0}, use_global_device_ids=true | all-gather | bytes 147456 | tf_op jit(solution)/shard_map/all_gather | solution.py:683
  130.7 0.6 slice_bitcast_fusion.2
  131.4 11.6 %all-to-all-done = bf16[8,152,256]{2,1,0:T(8,128)(2,1)S(1)} async-done(((bf16[8,152,256]{2,1,0:T(8,128)(2,1)}), bf16[8,152,256]{2,1,0:T(8,128)(2,1)S(1)}, u32[]{:S(2)}, u32[]{:S(2)}) %all-to-all-start) | async-done | bytes 622624 | tf_op jit(solution)/shard_map/all_to_all | solution.py:680
  143.1 0.6 slice.73
  143.7 0.6 fusion.3
  144.3 0.1 slice_reduce_fusion
  144.4 0.6 slice_bitcast_fusion
  (16 shorter events, 0.1 us)
Async XLA Ops:
  7.2 83.9 %all-gather.6.cloned.1.call-start = ((), (), s32[]{:S(2)}) async-start(), calls=%async_computation.1 | async-start | bytes 3342336 | tf_op jit(solution)/shard_map/all_gather | solution.py:645
  59.9 7.1 %collective-permute-start = (f32[18,512]{1,0:T(8,128)}, f32[18,512]{1,0:T(8,128)S(1)}, u32[]{:S(2)}, u32[]{:S(2)}) collective-permute-start(f32[18,512]{1,0:T(8,128)} %get-tuple-element.44), channel_id=1, source_target_pairs={{0,32},{32,0},{64,96},{96,64},{128,160},{160,128},{192,224},{224,1... | collective-permute-start | bytes 110600 | tf_op jit(solution)/shard_map/ppermute | solution.py:657
  79.9 6.7 %collective-permute-start.1 = (f32[9,512]{1,0:T(8,128)S(1)}, f32[9,512]{1,0:T(8,128)S(1)}, u32[]{:S(2)}, u32[]{:S(2)}) collective-permute-start(f32[9,512]{1,0:T(8,128)S(1)} %slice_select_fusion), channel_id=1, source_target_pairs={{0,64},{32,96},{64,0},{96,32},{128,192},{160,224},{192,128},{224,1... | collective-permute-start | bytes 55304 | tf_op jit(solution)/shard_map/ppermute | solution.py:661
  97.0 9.7 %collective-permute-start.2 = (bf16[4,128,256]{2,1,0:T(8,128)(2,1)}, bf16[4,128,256]{2,1,0:T(8,128)(2,1)S(1)}, u32[]{:S(2)}, u32[]{:S(2)}) collective-permute-start(bf16[4,128,256]{2,1,0:T(8,128)(2,1)} %get-tuple-element.53), channel_id=1, source_target_pairs={{0,32},{32,0},{64,96},{96,64},{128,160},{160,128},{192,224},{224,1... | collective-permute-start | bytes 786440 | tf_op jit(solution)/shard_map/ppermute | solution.py:673
  98.9 9.7 %collective-permute-start.3 = (bf16[4,128,256]{2,1,0:T(8,128)(2,1)}, bf16[4,128,256]{2,1,0:T(8,128)(2,1)S(1)}, u32[]{:S(2)}, u32[]{:S(2)}) collective-permute-start(bf16[4,128,256]{2,1,0:T(8,128)(2,1)} %get-tuple-element.55), channel_id=1, source_target_pairs={{0,480},{32,64},{64,32},{96,128},{128,96},{160,192},{192,160},{224... | collective-permute-start | bytes 786440 | tf_op jit(solution)/shard_map/ppermute | solution.py:673
  109.6 8.2 %copy-start = (f32[32,128]{1,0:T(8,128)S(1)}, f32[32,128]{1,0:T(8,128)}, u32[]{:S(2)}) copy-start(f32[32,128]{1,0:T(8,128)} %get-tuple-element.58) | copy-start | bytes 49156
  110.5 32.5 %all-to-all-start = ((bf16[8,152,256]{2,1,0:T(8,128)(2,1)}), bf16[8,152,256]{2,1,0:T(8,128)(2,1)S(1)}, u32[]{:S(2)}, u32[]{:S(2)}) async-start(bf16[8,152,256]{2,1,0:T(8,128)(2,1)} %pad_maximum_fusion), calls=%async_computation | async-start | bytes 1245184 | tf_op jit(solution)/shard_map/all_to_all | solution.py:680
Sparse Core Ops, SparseCore 0:
  10.1 80.9 all-gather.5

commit v5 on v4

--- a/solution.py
+++ b/solution.py
@@ -359,8 +359,8 @@
 def key_value_copies(all_hbm, kv_ref, width):
     return [
         (all_hbm.at[:, k, :, width + v : width + v + HEAD], kv_ref.at[k, :, :, v : v + HEAD])
+        for v in (0, HEAD)
         for k in range(2)
-        for v in (0, HEAD)
     ]
 
 
@@ -374,17 +374,16 @@
     return value.reshape(-1, HEAD)
 
 
-def gradients(k, kv_ref, probs, query, d_att, dout_t, rowdot, kv_grad_refs):
+def gradients(k, tokens, kv_ref, probs, query, d_att, dout_t, rowdot, kv_grad_refs):
     keys = keys_of(kv_ref, k)
     d_probs = dot(values_of(kv_ref, k), dout_t)
     d_scores = (probs * (d_probs - rowdot)).astype(BF16)
     key_grad = (dot(d_scores, query) * (HEAD ** -0.5)).astype(BF16)
     value_grad = dot(probs.astype(BF16), d_att).astype(BF16)
-    tokens = kv_grad_refs[0].shape[1]
     for m in range(keys.shape[0] // tokens):
         rows = slice(m * tokens, (m + 1) * tokens)
-        kv_grad_refs[m % 2][m // 2, :, :HEAD] = key_grad[rows]
-        kv_grad_refs[m % 2][m // 2, :, HEAD:] = value_grad[rows]
+        kv_grad_refs[m % 2][m // 2, :tokens, :HEAD] = key_grad[rows]
+        kv_grad_refs[m % 2][m // 2, :tokens, HEAD:] = value_grad[rows]
     return dot(keys.astype(F32).T.astype(BF16), d_scores)
 
 
@@ -414,7 +413,7 @@
         ))
     picks = begin_copies(picks, semaphores.at[5:])
     rest = begin_copies(
-        [(dout_hbm.at[0], dout_ref)] + key_value_copies(all_hbm, kv_ref, width), semaphores
+        key_value_copies(all_hbm, kv_ref, width) + [(dout_hbm.at[0], dout_ref)], semaphores
     )
 
     column = lax.rem(iota((1, columns), 1), tokens)
@@ -429,14 +428,11 @@
     bounds_ref[:1] = last
     bounds_ref[1:2] = opening
 
-    wait_all(rest[:1])
-    d_att = by_head(dout_ref)
-    dout_t[...] = d_att.astype(F32).T.astype(BF16)
     wait_all(picks)
     query = by_head(picked_ref)
     query_ref[...] = query
     query_t[...] = query.astype(F32).T.astype(BF16)
-    wait_all(rest[1:])
+    wait_all(rest[:2])
 
     top = jnp.full((8, columns), NEG, F32)
     for k in range(2):
@@ -447,6 +443,9 @@
         top = jnp.maximum(top, jnp.max(scores.reshape(half // 8, 8, columns), axis=0))
     shift = jnp.max(top, axis=0, keepdims=True) * factor
 
+    wait_all(rest[2:])
+    d_att = by_head(dout_ref)
+    dout_t[...] = d_att.astype(F32).T.astype(BF16)
     total = jnp.zeros((8, columns), F32)
     attended = jnp.zeros((HEAD, columns), F32)
     other = 1 - lax.rem(own_ref[0], 2)
@@ -465,15 +464,19 @@
 
     probs = weights * inverse
     query_acc[...] = gradients(
-        other, kv_ref, probs, query, d_att, dout_t[...], rowdot, (kv_near_ref, kv_far_ref)
+        other, tokens, kv_ref, probs, query, d_att, dout_t[...], rowdot,
+        (kv_near_ref, kv_far_ref),
     )
 
 
 def own_half_kernel(
-    own_ref, all_hbm, dout_hbm, stats_hbm, bounds_hbm, query_hbm, query_t_hbm, dout_t_hbm, acc_hbm,
-    query_grad_ref, kv_near_ref, kv_far_ref,
-    kv_ref, dout_ref, stats_ref, bounds_ref, query_ref, query_t, dout_t, query_acc, semaphores,
+    own_ref, all_hbm, dout_hbm, split_hbm, stats_hbm, bounds_hbm, query_hbm, query_t_hbm,
+    dout_t_hbm, acc_hbm,
+    query_grad_ref, sent_ref,
+    kv_ref, dout_ref, split_ref, stats_ref, bounds_ref, query_ref, query_t, dout_t, query_acc,
+    semaphores,
 ):
+    count = sent_ref.shape[0]
     tokens, width = dout_ref.shape
     half = kv_ref.shape[1] * tokens
     columns = width // HEAD * tokens
@@ -485,7 +488,7 @@
             (query_t_hbm, query_t), (bounds_hbm, bounds_ref), (stats_hbm, stats_ref),
             (all_hbm.at[:, own, :, width + HEAD :], kv_ref.at[0, :, :, HEAD:]),
             (dout_t_hbm, dout_t), (query_hbm, query_ref), (dout_hbm.at[0], dout_ref),
-            (acc_hbm, query_acc),
+            (acc_hbm, query_acc), (split_hbm, split_ref),
         ),
         semaphores,
     )
@@ -495,9 +498,11 @@
     valid = inside(own, tokens, bounds_ref[:1], bounds_ref[1:2], dims)
     probs = jnp.where(valid, jnp.exp2(scores * factor - stats_ref[:1]), 0.0)
     wait_all(copies[4:])
+    for m in range(count):
+        sent_ref[m, tokens:] = split_ref[...]
     part = gradients(
-        0, kv_ref, probs, query_ref[...], by_head(dout_ref), dout_t[...], stats_ref[1:2],
-        (kv_near_ref, kv_far_ref),
+        0, tokens, kv_ref, probs, query_ref[...], by_head(dout_ref), dout_t[...],
+        stats_ref[1:2], (sent_ref.at[: count // 2], sent_ref.at[count // 2 :]),
     )
     turn_back(query_grad_ref, (query_acc[...] + part) * (HEAD ** -0.5))
 
@@ -603,31 +608,29 @@
     return out, (near, far), carried
 
 
-def run_own_half(own, gathered, dout, carried):
+def run_own_half(own, gathered, dout, split, carried):
     tokens, width = dout.shape[1:]
     pairs = gathered.shape[0]
     columns = width // HEAD * tokens
-    kv_shape = shape(pairs // 2, tokens, 2 * HEAD, dtype=BF16)
-    query_grad, *kv_parts = pl.pallas_call(
+    return pl.pallas_call(
         own_half_kernel,
-        out_shape=(shape(tokens, width, dtype=BF16), kv_shape, kv_shape),
-        in_specs=[SMEM] + [HBM] * 8,
-        out_specs=[VMEM] * 3,
+        out_shape=(
+            shape(tokens, width, dtype=BF16),
+            shape(pairs, tokens + split.shape[0], 2 * HEAD, dtype=BF16),
+        ),
+        in_specs=[SMEM] + [HBM] * 9,
+        out_specs=[VMEM] * 2,
         scratch_shapes=[
             wide(1, pairs, tokens, 2 * HEAD, dtype=BF16), wide(tokens, width, dtype=BF16),
+            wide(*split.shape, dtype=BF16),
             wide(8, columns), wide(8, columns, dtype=jnp.int32),
             wide(columns, HEAD, dtype=BF16), wide(HEAD, columns, dtype=BF16),
             wide(HEAD, columns, dtype=BF16), wide(HEAD, columns),
-            pltpu.SemaphoreType.DMA((9,)),
+            pltpu.SemaphoreType.DMA((10,)),
         ],
         compiler_params=PARAMS,
-        cost_estimate=pl.CostEstimate(
-            flops=8 * pairs * tokens * columns * HEAD, bytes_accessed=4 * gathered.size,
-            transcendentals=pairs * tokens * columns,
-        ),
         name="attention_own_half",
-    )(own, gathered, dout, *carried)
-    return query_grad, kv_parts
+    )(own, gathered, dout, split, *carried)
 
 
 def on_device(
@@ -672,10 +675,9 @@
     arrived = [
         lax.ppermute(part, "seq", pairs) for part, pairs in zip(kv_other, (one_side, other_side))
     ]
-    query_gradient, kv_own = run_own_half(own, gathered, dout_in, carried)
-    kv_pair = [(a.astype(F32) + b.astype(F32)).astype(BF16) for a, b in zip(kv_own, arrived)]
-    split = jnp.broadcast_to(split[None], (seq_count // 2, *split.shape))
-    sent = jnp.concatenate([jnp.concatenate(kv_pair, 0), split], 1)
+    query_gradient, sent = run_own_half(own, gathered, dout_in, split, carried)
+    arrived = jnp.pad(jnp.concatenate(arrived, 0), ((0, 0), (0, split.shape[0]), (0, 0)))
+    sent = (sent.astype(F32) + arrived.astype(F32)).astype(BF16)
     sent, bc_part = lax.optimization_barrier((sent, bc_part))
     parts = lax.all_to_all(
         sent, "seq", split_axis=0, concat_axis=0, axis_index_groups=same_parity

time: 152 us -> 154 us (1.013)
  the two profiles are of different devices: /device:TPU:98 before, /device:TPU:56 now
where the time goes in v5:
time: 154 us; the launch traced here: 153 us
  blocking collectives  66.7 us (43%)
  starting transfers between devices  23 us (15%)
  Pallas kernels  22.9 us (15%)
  waiting for transfers between devices  18.7 us (12%)
  between operations  14.2 us (9%)
  other arithmetic  5.22 us (3%)
  local copies, waits for them, and re-layouts  2.5 us (2%)
    all_gather x1, blocking collectives, on_device(): summaries = lax.all_gather(summary, 'seq', axis=0)  41.2 us
    all_gather x1, blocking collectives, on_device(): bc_sum = jnp.sum(lax.all_gather(bc_part, 'tp', axis=0), axis=0)  12.8 us
    all_gather x1, blocking collectives, on_device(): params = jnp.sum(lax.all_gather(params, 'dp', axis=0), axis=0)  12.7 us
    all_to_all x1, starting transfers between devices, on_device(): lax.all_to_all(sent, 'seq', split_axis=0, concat_axis=0, axis_index_group...  10.5 us
    all_to_all x1, waiting for transfers between devices, on_device(): lax.all_to_all(sent, 'seq', split_axis=0, concat_axis=0, axis_index_group...  9.16 us
    pallas_call x1, Pallas kernels, run_mixer(): pl.pallas_call(mixer_kernel, out_shape=(shape(tokens, width, dtype=BF16),...  7.92 us
    ppermute x2, starting transfers between devices, on_device(): lax.ppermute(part, 'seq', pairs)  6.72 us
    pallas_call x1, Pallas kernels, run_attention(): pl.pallas_call(attention_kernel, out_shape=(shape(tokens, width, dtype=BF...  5.72 us
  transfers between devices with their start and end apart: 6, of which 4 were waited for; matrix products, arithmetic and copies ran while one was open for 1% of the time, Pallas kernels for 11%

profile of v5, /device:TPU:56, one launch (start us, length us, event | category | flops | bytes accessed | tf_op | source)
XLA Modules:
  0.0 153.3 jit_solution(6920317620109220381)
XLA Ops:
  7.2 0.0 all-gather.6.cloned.1.call-start
  7.2 1.6 %pad_maximum_fusion = bf16[128,768]{1,0:T(8,128)(2,1)} fusion(bf16[128,128]{1,0:T(8,128)(2,1)} %bitcast.40, bf16[128,128]{1,0:T(8,128)(2,1)} %bitcast.41, bf16[128,512]{1,0:T(8,128)(2,1)} %bitcast.39), kind=kLoop, calls=%fused_computation.6 | loop fusion | flops 589824 | bytes 393216 | tf_op jit(solution)/shard_map/concatenate | solution.py:647
  8.9 0.0 all-gather.6.cloned.1.call-update
  8.9 5.3 %mixer_summary.1 = (bf16[136,128]{1,0:T(8,128)(2,1)}, f32[16,8,512]{2,1,0:T(8,128)}, f32[16,8,512]{2,1,0:T(8,128)}, f32[8,512]{1,0:T(8,128)}) custom-call(s32[1]{0:T(128)} %bitcast.own_ref, s32[1,8]{1,0:T(1,128)} %lengths_ref.1, bf16[1,128,512]{2,1,0:T(8,128)(2,1)} %x_hbm.3, bf16[1,128,512]{2,1,0:T(8,128)(2,1)} %dt_hbm.3, bf16[1,128,512]{2,1,0:T(8,128)(2,1)} %dy_hbm.3, ...), custom_call_target="tpu_custom_call" | custom-call | tf_op jit(solution)/shard_map/mixer_summary/pallas_call | solution.py:526
  14.2 41.2 %all-gather = bf16[2176,128]{1,0:T(8,128)(2,1)} all-gather(bf16[136,128]{1,0:T(8,128)(2,1)} %get-tuple-element.36), channel_id=2, replica_groups=mesh['seq'=16,'tp'=8,'dp'=4] {'seq'}, dimensions={0}, use_global_device_ids=true | all-gather | bytes 591872 | tf_op jit(solution)/shard_map/all_gather | solution.py:651
  55.4 7.9 %mixer.1 = (bf16[128,512]{1,0:T(8,128)(2,1)}, bf16[128,512]{1,0:T(8,128)(2,1)}, bf16[128,512]{1,0:T(8,128)(2,1)}, f32[32,128]{1,0:T(8,128)}, f32[18,512]{1,0:T(8,128)}) custom-call(s32[1]{0:T(128)} %bitcast.own_ref, s32[1,8]{1,0:T(1,128)} %lengths_ref.1, bf16[1,128,512]{2,1,0:T(8,128)(2,1)} %x_hbm.3, bf16[1,128,512]{2,1,0:T(8,128)(2,1)} %dt_hbm.3, ...), custom_call_target="tpu_custom_call" | custom-call | tf_op jit(solution)/shard_map/mixer/pallas_call | solution.py:552
  63.4 3.4 %collective-permute-start = (f32[18,512]{1,0:T(8,128)}, f32[18,512]{1,0:T(8,128)S(1)}, u32[]{:S(2)}, u32[]{:S(2)}) collective-permute-start(f32[18,512]{1,0:T(8,128)} %get-tuple-element.43), channel_id=1, source_target_pairs={{0,32},{32,0},{64,96},{96,64},{128,160},{160,128},{192,224},{224,1... | collective-permute-start | bytes 110600 | tf_op jit(solution)/shard_map/ppermute | solution.py:660
  66.8 3.6 %collective-permute-done = f32[18,512]{1,0:T(8,128)S(1)} collective-permute-done((f32[18,512]{1,0:T(8,128)}, f32[18,512]{1,0:T(8,128)S(1)}, u32[]{:S(2)}, u32[]{:S(2)}) %collective-permute-start) | collective-permute-done | bytes 36896 | tf_op jit(solution)/shard_map/ppermute | solution.py:660
  70.3 0.8 add_bitcast_fusion
  71.1 12.7 %all-gather.3 = f32[4,18,512]{2,1,0:T(8,128)S(1)} all-gather(f32[1,18,512]{2,1,0:T(8,128)S(1)} %add_bitcast_fusion), channel_id=3, replica_groups=mesh['seq'=16,'tp'=8,'dp'=4] {'dp'}, dimensions={0}, use_global_device_ids=true | all-gather | bytes 184320 | tf_op jit(solution)/shard_map/all_gather | solution.py:661
  83.9 2.4 %collective-permute-start.1 = (f32[9,512]{1,0:T(8,128)S(1)}, f32[9,512]{1,0:T(8,128)S(1)}, u32[]{:S(2)}, u32[]{:S(2)}) collective-permute-start(f32[9,512]{1,0:T(8,128)S(1)} %slice_select_fusion), channel_id=1, source_target_pairs={{0,64},{32,96},{64,0},{96,32},{128,192},{160,224},{192,128},{224,1... | collective-permute-start | bytes 55304 | tf_op jit(solution)/shard_map/ppermute | solution.py:664
  86.3 4.3 %collective-permute-done.1 = f32[9,512]{1,0:T(8,128)S(1)} collective-permute-done((f32[9,512]{1,0:T(8,128)S(1)}, f32[9,512]{1,0:T(8,128)S(1)}, u32[]{:S(2)}, u32[]{:S(2)}) %collective-permute-start.1) | collective-permute-done | bytes 18464 | tf_op jit(solution)/shard_map/ppermute | solution.py:664
  90.6 0.6 fusion.5.split_hbm
  91.2 0.0 all-gather.6.cloned.1.call-done
  91.3 5.7 %attention.1 = (bf16[128,512]{1,0:T(8,128)(2,1)}, bf16[4,128,256]{2,1,0:T(8,128)(2,1)}, bf16[4,128,256]{2,1,0:T(8,128)(2,1)}, f32[8,512]{1,0:T(8,128)}, s32[8,51...) custom-call(s32[1]{0:T(128)} %bitcast.own_ref, ...), custom_call_target="tpu_custom_call" | custom-call | flops 671088640 | bytes 12582912 | tf_op jit(solution)/shard_map/attention/pallas_call | solution.py:586
  97.0 3.9 %collective-permute-start.2 = (bf16[4,128,256]{2,1,0:T(8,128)(2,1)}, bf16[4,128,256]{2,1,0:T(8,128)(2,1)S(1)}, u32[]{:S(2)}, u32[]{:S(2)}) collective-permute-start(bf16[4,128,256]{2,1,0:T(8,128)(2,1)} %get-tuple-element.53), channel_id=1, source_target_pairs={{0,32},{32,0},{64,96},{96,64},{128,160},{160,128},{192,224},{224,1... | collective-permute-start | bytes 786440 | tf_op jit(solution)/shard_map/ppermute | solution.py:676
  100.9 2.8 %collective-permute-start.3 = (bf16[4,128,256]{2,1,0:T(8,128)(2,1)}, bf16[4,128,256]{2,1,0:T(8,128)(2,1)S(1)}, u32[]{:S(2)}, u32[]{:S(2)}) collective-permute-start(bf16[4,128,256]{2,1,0:T(8,128)(2,1)} %get-tuple-element.54), channel_id=1, source_target_pairs={{0,480},{32,64},{64,32},{96,128},{128,96},{160,192},{192,160},{224... | collective-permute-start | bytes 786440 | tf_op jit(solution)/shard_map/ppermute | solution.py:676
  103.7 4.0 %attention_own_half.1 = (bf16[128,512]{1,0:T(8,128)(2,1)}, bf16[8,152,256]{2,1,0:T(8,128)(2,1)}) custom-call(s32[1]{0:T(128)} %bitcast.own_ref, bf16[8,2,128,768]{3,2,1,0:T(8,128)(2,1)} %bitcast.35, bf16[1,128,512]{2,1,0:T(8,128)(2,1)} %dout_hbm.3, bf16[24,256]{1,0:T(8,128)(2,1)} %fusion.5.split_hbm, f32[8,512]{1,0:T(8,128)} %get-tuple-element.46.stats_hbm, ...), custom_call_target="tpu_custom_call" | custom-call | tf_op jit(solution)/shard_map/attention_own_half/pallas_call | solution.py:615
  107.7 0.0 collective-permute-done.2
  107.7 1.6 %collective-permute-done.3 = bf16[4,128,256]{2,1,0:T(8,128)(2,1)S(1)} collective-permute-done((bf16[4,128,256]{2,1,0:T(8,128)(2,1)}, bf16[4,128,256]{2,1,0:T(8,128)(2,1)S(1)}, u32[]{:S(2)}, u32[]{:S(2)}) %collective-permute-start.3) | collective-permute-done | bytes 262176 | tf_op jit(solution)/shard_map/ppermute | solution.py:676
  109.4 0.0 copy-start
  109.4 2.0 %add_convert_fusion = bf16[8,152,256]{2,1,0:T(8,128)(2,1)} fusion(bf16[8,152,256]{2,1,0:T(8,128)(2,1)} %get-tuple-element.52, bf16[4,128,256]{2,1,0:T(8,128)(2,1)S(1)} %collective-permute-done.3, bf16[4,128,256]{2,1,0:T(8,128)(2,1)S(1)} %collective-permute-done.2), kind=kLoop, calls=%fused_computation.3 | loop fusion | flops 3112960 | bytes 1769472 | tf_op jit(solution)/shard_map/convert_element_type | solution.py:680
  111.4 10.5 %all-to-all-start = ((bf16[8,152,256]{2,1,0:T(8,128)(2,1)}), bf16[8,152,256]{2,1,0:T(8,128)(2,1)S(1)}, u32[]{:S(2)}, u32[]{:S(2)}) async-start(bf16[8,152,256]{2,1,0:T(8,128)(2,1)} %add_convert_fusion), calls=%async_computation | async-start | bytes 1245184 | tf_op jit(solution)/shard_map/all_to_all | solution.py:682
  121.9 0.0 copy-done
  121.9 12.8 %all-gather.2 = f32[256,128]{1,0:T(8,128)S(1)} all-gather(f32[32,128]{1,0:T(8,128)S(1)} %copy-done), channel_id=4, replica_groups=mesh['seq'=16,'tp'=8,'dp'=4] {'tp'}, dimensions={0}, use_global_device_ids=true | all-gather | bytes 147456 | tf_op jit(solution)/shard_map/all_gather | solution.py:685
  134.7 0.6 slice_bitcast_fusion.2
  135.3 9.2 %all-to-all-done = bf16[8,152,256]{2,1,0:T(8,128)(2,1)S(1)} async-done(((bf16[8,152,256]{2,1,0:T(8,128)(2,1)}), bf16[8,152,256]{2,1,0:T(8,128)(2,1)S(1)}, u32[]{:S(2)}, u32[]{:S(2)}) %all-to-all-start) | async-done | bytes 622624 | tf_op jit(solution)/shard_map/all_to_all | solution.py:682
  144.6 0.6 fusion.6
  145.1 0.6 slice.73
  145.8 0.1 slice_reduce_fusion
  145.8 0.6 slice_bitcast_fusion
  (14 shorter events, 0.1 us)
Async XLA Ops:
  7.2 84.1 %all-gather.6.cloned.1.call-start = ((), (), s32[]{:S(2)}) async-start(), calls=%async_computation.1 | async-start | bytes 3342336 | tf_op jit(solution)/shard_map/all_gather | solution.py:648
  63.4 7.0 %collective-permute-start = (f32[18,512]{1,0:T(8,128)}, f32[18,512]{1,0:T(8,128)S(1)}, u32[]{:S(2)}, u32[]{:S(2)}) collective-permute-start(f32[18,512]{1,0:T(8,128)} %get-tuple-element.43), channel_id=1, source_target_pairs={{0,32},{32,0},{64,96},{96,64},{128,160},{160,128},{192,224},{224,1... | collective-permute-start | bytes 110600 | tf_op jit(solution)/shard_map/ppermute | solution.py:660
  83.9 6.7 %collective-permute-start.1 = (f32[9,512]{1,0:T(8,128)S(1)}, f32[9,512]{1,0:T(8,128)S(1)}, u32[]{:S(2)}, u32[]{:S(2)}) collective-permute-start(f32[9,512]{1,0:T(8,128)S(1)} %slice_select_fusion), channel_id=1, source_target_pairs={{0,64},{32,96},{64,0},{96,32},{128,192},{160,224},{192,128},{224,1... | collective-permute-start | bytes 55304 | tf_op jit(solution)/shard_map/ppermute | solution.py:664
  97.0 10.7 %collective-permute-start.2 = (bf16[4,128,256]{2,1,0:T(8,128)(2,1)}, bf16[4,128,256]{2,1,0:T(8,128)(2,1)S(1)}, u32[]{:S(2)}, u32[]{:S(2)}) collective-permute-start(bf16[4,128,256]{2,1,0:T(8,128)(2,1)} %get-tuple-element.53), channel_id=1, source_target_pairs={{0,32},{32,0},{64,96},{96,64},{128,160},{160,128},{192,224},{224,1... | collective-permute-start | bytes 786440 | tf_op jit(solution)/shard_map/ppermute | solution.py:676
  100.9 8.5 %collective-permute-start.3 = (bf16[4,128,256]{2,1,0:T(8,128)(2,1)}, bf16[4,128,256]{2,1,0:T(8,128)(2,1)S(1)}, u32[]{:S(2)}, u32[]{:S(2)}) collective-permute-start(bf16[4,128,256]{2,1,0:T(8,128)(2,1)} %get-tuple-element.54), channel_id=1, source_target_pairs={{0,480},{32,64},{64,32},{96,128},{128,96},{160,192},{192,160},{224... | collective-permute-start | bytes 786440 | tf_op jit(solution)/shard_map/ppermute | solution.py:676
  109.4 12.5 %copy-start = (f32[32,128]{1,0:T(8,128)S(1)}, f32[32,128]{1,0:T(8,128)}, u32[]{:S(2)}) copy-start(f32[32,128]{1,0:T(8,128)} %get-tuple-element.56) | copy-start | bytes 49156
  111.4 33.0 %all-to-all-start = ((bf16[8,152,256]{2,1,0:T(8,128)(2,1)}), bf16[8,152,256]{2,1,0:T(8,128)(2,1)S(1)}, u32[]{:S(2)}, u32[]{:S(2)}) async-start(bf16[8,152,256]{2,1,0:T(8,128)(2,1)} %add_convert_fusion), calls=%async_computation | async-start | bytes 1245184 | tf_op jit(solution)/shard_map/all_to_all | solution.py:682
Sparse Core Ops, SparseCore 0:
  10.1 80.8 all-gather.5
